TPU v7x, 128 devices: a whole 4x4x4 slice. The times are simulated.
128 devices in a mesh: gx: 8 (over z, core), gy: 16 (over x, y).
Axes of the slice: x: 4, y: 4, z: 4, core: 2. Of those that a mesh axis runs over, the one named last changes fastest.
Arguments:
- jac_cam: float32 [8, 16, 128, 18, 128], P('gx', 'gy'), may hold values from -6 to 6
- jac_pt: float32 [8, 16, 128, 6, 128], P('gx', 'gy'), may hold values from -6 to 6
- resid0: float32 [8, 16, 128, 2, 128], P('gx', 'gy'), may hold values from -40 to 40
- obs_count: int32 [8, 16, 128], P('gx', 'gy'), may hold values from 0 to 128, as said below
- tile_camera: int32 [8, 16, 128], P('gx', 'gy'), may hold values from 0 to 3
- tile_points: int32 [8, 16, 128], P('gx', 'gy'), may hold values from 0 to 143, as said below
- obs_camera: int32 [8, 16, 128, 128], P('gx', 'gy'), may hold values from 0 to 63
- obs_point: int32 [8, 16, 128, 128], P('gx', 'gy'), may hold values from 0 to 127
- cam_params: float32 [8, 16, 4, 9, 64], P('gx', 'gy'), may hold values from -6 to 6
- pt_params: float32 [8, 16, 16, 3, 128], P('gx', 'gy'), may hold values from -6 to 6
- cg_start: float32 [8, 16, 4, 9, 64], P('gx', 'gy'), may hold values from -1.5 to 1.5
Outputs:
- cam_out: float32 [8, 16, 4, 9, 64], P('gx', 'gy')
- pt_out: float32 [8, 16, 16, 3, 128], P('gx', 'gy')
- resid_out: float32 [8, 16, 128, 2, 128], P('gx', 'gy')
- costs: float32 [3], replicated
Inputs may be any that keep to these rules, and one draw needn't show every extreme that they name: `obs_count`: on each device the tiles that hold observations come first, 16 or more of them, each with 64 or more observations in its first slots; some device has no tile without observations. `tile_points`: A slot (3 a + b) * 16 + q stands for point block q of the device a - 1 steps along gx and b - 1 steps along gy; it never names a device outside the grid.
All inputs are finite; a program needn't handle non-finite values.
Results may differ from a plain program's by a relative error of at most 0.0001.
Values sent between devices are 32-bit elements; how exact they have to be, the bound alone decides.
A program may use at most 64 MiB of HBM per device.

v0:
```python
import jax
import jax.numpy as jnp
from jax import lax
from jax.sharding import PartitionSpec as P

LM_STEPS = 2
CG_ITERS = 2


precise = lax.Precision.HIGHEST
damping_first = 1.0
damping_ratio = 0.25
hess_pairs = ((0, 0), (0, 1), (0, 2), (1, 1), (1, 2), (2, 2))


def with_halo(array, sides, width):
    for axis, dim in sides:
        peers, length = (lax.axis_size(axis), array.shape[dim])
        up = [(i, (i + 1) % peers) for i in range(peers - 1)]
        down = [(j, i) for i, j in up]
        last = lax.slice_in_dim(array, length - width, length, axis=dim)
        first = lax.slice_in_dim(array, 0, width, axis=dim)
        before = lax.ppermute(last, axis, up)
        after = lax.ppermute(first, axis, down)
        array = jnp.concatenate([before, array, after], axis=dim)
    return array


def passed_along(value, axis, steps):
    count = lax.axis_size(axis)
    first, last = (max(0, -steps), min(count, count - steps))
    return lax.ppermute(value, axis, [(source, source + steps) for source in range(first, last)])


def damped_inverse_apply(hess_cols, vector, damping):
    h_zero = hess_cols[0] + damping * (hess_cols[0] + 1.0)
    h_zero_one = hess_cols[1]
    h_zero_two = hess_cols[2]
    h_one = hess_cols[3] + damping * (hess_cols[3] + 1.0)
    h_one_two = hess_cols[4]
    h_two = hess_cols[5] + damping * (hess_cols[5] + 1.0)
    cof_zero = h_one * h_two - h_one_two * h_one_two
    cof_zero_one = h_zero_two * h_one_two - h_zero_one * h_two
    cof_zero_two = h_zero_one * h_one_two - h_zero_two * h_one
    cof_one = h_zero * h_two - h_zero_two * h_zero_two
    cof_one_two = h_zero_one * h_zero_two - h_zero * h_one_two
    cof_two = h_zero * h_one - h_zero_one * h_zero_one
    determ = h_zero * cof_zero + h_zero_one * cof_zero_one + h_zero_two * cof_zero_two
    out_zero = (cof_zero * vector[0] + cof_zero_one * vector[1] + cof_zero_two * vector[2]) / determ
    out_one = (cof_zero_one * vector[0] + cof_one * vector[1] + cof_one_two * vector[2]) / determ
    out_two = (cof_zero_two * vector[0] + cof_one_two * vector[1] + cof_two * vector[2]) / determ
    return (out_zero, out_one, out_two)


def in_blocks(block_fn, arrays):
    row_total = arrays[0].shape[0]
    block_rows = 32
    shaped = tuple(
        (
            member.reshape((row_total // block_rows, block_rows) + member.shape[1:])
            for member in arrays
        )
    )
    result = lax.map(lambda members: block_fn(*members), shaped)
    return result.reshape((row_total,) + result.shape[2:])


def one_hot_table(indices, table_size):
    return (indices[:, None, :] == lax.broadcasted_iota(jnp.int32, (1, table_size, 1), 1)).astype(
        jnp.float32
    )


def body(
    jac_cam,
    jac_pt,
    resid0,
    obs_count,
    tile_camera,
    tile_points,
    obs_camera,
    obs_point,
    cam_params,
    pt_params,
    cg_start,
):
    tile_total = resid0.shape[2]
    slot_total = resid0.shape[4]
    camera_now = cam_params[0, 0]
    cam_blocks, cam_width, cam_count = camera_now.shape
    point_now = pt_params[0, 0]
    point_blocks = point_now.shape[0]
    point_count = point_now.shape[2]
    valid = (
        lax.broadcasted_iota(jnp.int32, (tile_total, slot_total), 1) < obs_count[0, 0][:, None]
    ).astype(jnp.float32)
    camera_jac = (jac_cam[0, 0] * valid[:, None, :]).reshape(tile_total, 2, cam_width, slot_total)
    point_jac = (jac_pt[0, 0] * valid[:, None, :]).reshape(tile_total, 2, 3, slot_total)
    resid = resid0[0, 0] * valid[:, None, :]
    camera_of = obs_camera[0, 0]
    point_of = obs_point[0, 0]
    tile_cams = (
        tile_camera[0, 0][:, None] == lax.broadcasted_iota(jnp.int32, (tile_total, cam_blocks), 1)
    ).astype(jnp.float32)
    tile_slots = (
        tile_points[0, 0][None, :]
        == lax.broadcasted_iota(jnp.int32, (9 * point_blocks, tile_total), 0)
    ).astype(jnp.float32)

    def gather_cams(values, indices):
        return jnp.einsum(
            "tkc,tco->tko", values, one_hot_table(indices, cam_count), precision=precise
        )

    def scatter_cams(values, indices):
        return jnp.einsum(
            "tko,tco->tkc", values, one_hot_table(indices, cam_count), precision=precise
        )

    def gather_points(values, indices):
        return jnp.einsum(
            "tmp,tpo->tmo", values, one_hot_table(indices, point_count), precision=precise
        )

    def scatter_points(values, indices):
        return jnp.einsum(
            "tmo,tpo->tmp", values, one_hot_table(indices, point_count), precision=precise
        )

    def take_cams(vector):
        per_tile = jnp.einsum("tb,bkc->tkc", tile_cams, vector, precision=precise)
        return in_blocks(gather_cams, (per_tile, camera_of))

    def put_cams(values):
        per_tile = in_blocks(scatter_cams, (values, camera_of))
        return jnp.einsum("tb,tkc->bkc", tile_cams, per_tile, precision=precise)

    def take_points(nearby):
        per_tile = jnp.einsum("st,smp->tmp", tile_slots, nearby, precision=precise)
        return in_blocks(gather_points, (per_tile, point_of))

    def put_points(values):
        per_tile = in_blocks(scatter_points, (values, point_of))
        return jnp.einsum("st,tmp->smp", tile_slots, per_tile, precision=precise)

    def spread(owned):
        rimmed = with_halo(owned[None, None], (("gx", 0), ("gy", 1)), 1)
        return rimmed.reshape((9 * owned.shape[0],) + owned.shape[1:])

    def collect(contributions):
        slot_grid = contributions.reshape((3, 3, point_blocks) + contributions.shape[1:])
        middle = (
            slot_grid[1]
            + passed_along(slot_grid[2], "gx", 1)
            + passed_along(slot_grid[0], "gx", -1)
        )
        return middle[1] + passed_along(middle[2], "gy", 1) + passed_along(middle[0], "gy", -1)

    def apply_cam(values):
        return jnp.sum(camera_jac * values[:, None, :, :], axis=2)

    def to_points(moved):
        return jnp.sum(point_jac * moved[:, :, None, :], axis=1)

    cam_diag = put_cams(jnp.sum(camera_jac * camera_jac, axis=1))
    hess_terms = jnp.stack(
        [
            jnp.sum(point_jac[:, :, row_pos, :] * point_jac[:, :, col_pos, :], axis=1)
            for row_pos, col_pos in hess_pairs
        ],
        axis=1,
    )
    point_hess = collect(put_points(hess_terms))
    hess_cols = tuple((point_hess[:, column] for column in range(6)))

    def reduced(moved, damping):
        owned = collect(put_points(to_points(moved)))
        solved = damped_inverse_apply(hess_cols, (owned[:, 0], owned[:, 1], owned[:, 2]), damping)
        nearby = take_points(spread(jnp.stack(solved, axis=1)))
        back = moved - jnp.sum(point_jac * nearby[:, None, :, :], axis=2)
        return put_cams(jnp.sum(camera_jac * back[:, :, None, :], axis=1))

    start = cg_start[0, 0]
    costs_list = []
    for lm_step in range(LM_STEPS + 1):
        cost_local = 0.5 * jnp.sum(resid * resid)
        costs_list.append(lax.psum(cost_local, ("gx", "gy")))
        if lm_step < LM_STEPS:
            damping = damping_first * damping_ratio**lm_step
            cam_damp = damping * (cam_diag + 1.0)
            precond = cam_diag + cam_damp
            moved = resid + apply_cam(take_cams(start))
            cg_resid = -reduced(moved, damping) - cam_damp * start
            scaled = cg_resid / precond
            direction = scaled
            local_dot = jnp.sum(cg_resid * scaled)
            resid_dot = lax.psum(local_dot, ("gx", "gy"))
            update = start
            for cg_turn in range(CG_ITERS):
                curved = reduced(apply_cam(take_cams(direction)), damping) + cam_damp * direction
                step_size = resid_dot / lax.psum(jnp.sum(direction * curved), ("gx", "gy"))
                update = update + step_size * direction
                cg_resid = cg_resid - step_size * curved
                if cg_turn + 1 < CG_ITERS:
                    scaled = cg_resid / precond
                    fresh = lax.psum(jnp.sum(cg_resid * scaled), ("gx", "gy"))
                    direction = scaled + fresh / resid_dot * direction
                    resid_dot = fresh
            moved = resid + apply_cam(take_cams(update))
            owned = collect(put_points(to_points(moved)))
            solved = damped_inverse_apply(
                hess_cols, (owned[:, 0], owned[:, 1], owned[:, 2]), damping
            )
            point_step = -jnp.stack(solved, axis=1)
            resid = moved + jnp.sum(
                point_jac * take_points(spread(point_step))[:, None, :, :], axis=2
            )
            camera_now = camera_now + update
            point_now = point_now + point_step
            start = update
    return (camera_now[None, None], point_now[None, None], resid[None, None], jnp.stack(costs_list))


def solution(mesh):
    in_specs = (
        P("gx", "gy", None, None, None),
        P("gx", "gy", None, None, None),
        P("gx", "gy", None, None, None),
        P("gx", "gy", None),
        P("gx", "gy", None),
        P("gx", "gy", None),
        P("gx", "gy", None, None),
        P("gx", "gy", None, None),
        P("gx", "gy", None, None, None),
        P("gx", "gy", None, None, None),
        P("gx", "gy", None, None, None),
    )
    out_specs = (
        P("gx", "gy", None, None, None),
        P("gx", "gy", None, None, None),
        P("gx", "gy", None, None, None),
        P(),
    )
    return jax.shard_map(body, mesh=mesh, in_specs=in_specs, out_specs=out_specs, check_vma=False)
```

profile of v0, /device:TPU:1, one launch (start us, length us, event | category | flops | bytes accessed | tf_op | source)
XLA Modules:
  0.0 961.7 jit_solution(4008741901610615356)
XLA Ops:
  9.1 7.1 while.316
  16.5 4.9 collective-permute-start.4
  24.8 7.0 while.315
  54.1 5.6 collective-permute-start.8
  74.4 4.4 while.317
  80.3 6.7 while.318
  88.1 6.7 while.319
  101.4 7.1 while.321
  117.6 5.7 collective-permute-start.14
  141.6 4.0 collective-permute-done.19
  146.1 4.4 while.322
  155.9 67.7 %all-reduce.2 = (f32[]{:T(128)}, f32[]{:T(128)}) all-reduce(f32[]{:T(128)} %get-tuple-element.980, f32[]{:T(128)} %get-tuple-element.979), channel_id=1, replica_groups=mesh['gx'=8,'gy'=16] {'gx','gy'}, use_global_device_ids=true, to_apply=%region_24.25 | all-reduce | flops 2 | bytes 16 | tf_op jit(solution)/shard_map/psum | solution.py:197
  225.5 63.2 %psum.79 = f32[]{:T(128)} all-reduce(f32[]{:T(128)} %get-tuple-element.1250), channel_id=1, replica_groups=mesh['gx'=8,'gy'=16] {'gx','gy'}, use_global_device_ids=true, to_apply=%region_40.41 | all-reduce | flops 1 | bytes 8 | tf_op jit(solution)/shard_map/psum | solution.py:206
  294.0 7.1 while.325
  333.6 4.4 while.326
  343.5 68.1 %psum.80 = f32[]{:T(128)} all-reduce(f32[]{:T(128)} %fusion.111), channel_id=1, replica_groups=mesh['gx'=8,'gy'=16] {'gx','gy'}, use_global_device_ids=true, to_apply=%region_54.55 | all-reduce | flops 1 | bytes 8 | tf_op jit(solution)/shard_map/psum | solution.py:201
  418.2 7.1 while.329
  458.2 4.4 while.330
  464.1 7.1 while.331
  480.3 5.7 collective-permute-start.38
  510.4 4.4 while.332
  525.4 7.1 while.335
  558.5 4.0 collective-permute-start.50
  568.2 4.4 while.336
  578.7 66.9 %all-reduce.1 = (f32[]{:T(128)}, f32[]{:T(128)}) all-reduce(f32[]{:T(128)} %get-tuple-element.978, f32[]{:T(128)} %get-tuple-element.977), channel_id=1, replica_groups=mesh['gx'=8,'gy'=16] {'gx','gy'}, use_global_device_ids=true, to_apply=%region_74.75 | all-reduce | flops 2 | bytes 16 | tf_op jit(solution)/shard_map/psum | solution.py:197
  648.3 63.1 %psum.83 = f32[]{:T(128)} all-reduce(f32[]{:T(128)} %get-tuple-element.1238), channel_id=1, replica_groups=mesh['gx'=8,'gy'=16] {'gx','gy'}, use_global_device_ids=true, to_apply=%region_90.91 | all-reduce | flops 1 | bytes 8 | tf_op jit(solution)/shard_map/psum | solution.py:206
  717.3 7.1 while.339
  757.0 4.4 while.340
  767.6 68.3 %psum.84 = f32[]{:T(128)} all-reduce(f32[]{:T(128)} %fusion.114), channel_id=1, replica_groups=mesh['gx'=8,'gy'=16] {'gx','gy'}, use_global_device_ids=true, to_apply=%region_104.105 | all-reduce | flops 1 | bytes 8 | tf_op jit(solution)/shard_map/psum | solution.py:201
  842.5 7.1 while.343
  882.7 4.4 while.344
  889.5 69.6 %all-reduce = (f32[1]{0:T(128)}, f32[1]{0:T(128)}, f32[1]{0:T(128)}) all-reduce(f32[1]{0:T(128)} %bitcast.260, f32[1]{0:T(128)} %bitcast.259, f32[1]{0:T(128)} %bitcast.258), channel_id=1, replica_groups=mesh['gx'=8,'gy'=16] {'gx','gy'}, use_global_device_ids=true, to_apply=%region_119.120 | all-reduce | flops 3 | bytes 24 | tf_op jit(solution)/shard_map/psum | solution.py:187
  (909 shorter events, 488.2 us)
Async XLA Ops:
  16.5 21.3 %collective-permute-start.4 = (f32[3,16,3,128]{3,1,2,0:T(8,128)S(1)}, f32[3,16,3,128]{3,1,2,0:T(8,128)}, u32[]{:S(2)}, u32[]{:S(2)}) collective-permute-start(f32[3,16,3,128]{3,1,2,0:T(8,128)S(1)} %copy.204), channel_id=1, source_target_pairs={{0,16},{16,32},{32,48},{48,64},{64,80},{80,96},{96,112},{1,17},{17... | collective-permute-start | bytes 221192 | tf_op jit(solution)/shard_map/ppermute | solution.py:32
  22.1 15.7 %collective-permute-start.5 = (f32[3,16,3,128]{3,1,2,0:T(8,128)}, f32[3,16,3,128]{3,1,2,0:T(8,128)}, u32[]{:S(2)}, u32[]{:S(2)}) collective-permute-start(f32[3,16,3,128]{3,1,2,0:T(8,128)} %copy.206), channel_id=1, source_target_pairs={{16,0},{32,16},{48,32},{64,48},{80,64},{96,80},{112,96},{17,1},{33... | collective-permute-start | bytes 221192 | tf_op jit(solution)/shard_map/ppermute | solution.py:32
  32.2 11.1 %collective-permute-start = (f32[3,16,6,128]{3,1,2,0:T(8,128)S(1)}, f32[3,16,6,128]{3,1,2,0:T(8,128)S(1)}, u32[]{:S(2)}, u32[]{:S(2)}) collective-permute-start(f32[3,16,6,128]{3,1,2,0:T(8,128)S(1)} %copy.199), channel_id=1, source_target_pairs={{0,16},{16,32},{32,48},{48,64},{64,80},{80,96},{96,112},{1,17},{17... | collective-permute-start | bytes 442376 | tf_op jit(solution)/shard_map/ppermute | solution.py:32
  35.9 7.4 collective-permute-start.1
  38.8 9.9 %collective-permute-start.6 = (f32[16,3,128]{2,0,1:T(8,128)S(1)}, f32[16,3,128]{2,0,1:T(8,128)S(1)}, u32[]{:S(2)}, u32[]{:S(2)}) collective-permute-start(f32[16,3,128]{2,0,1:T(8,128)S(1)} %get-tuple-element.1309), channel_id=1, source_target_pairs={{0,1},{1,2},{2,3},{3,4},{4,5},{5,6},{6,7},{7,8},{8,9},{9,10},{10,1... | collective-permute-start | bytes 73736 | tf_op jit(solution)/shard_map/ppermute | solution.py:32
  42.0 6.7 collective-permute-start.7
  43.4 5.3 collective-permute-start.2
  54.1 7.6 collective-permute-start.8
  64.9 5.8 collective-permute-start.10
  68.1 5.9 collective-permute-start.11
  111.9 5.7 collective-permute-start.13
  117.6 7.1 collective-permute-start.14
  131.4 5.1 collective-permute-start.17
  140.3 5.4 collective-permute-start.19
  304.5 5.7 collective-permute-start.21
  316.5 5.2 collective-permute-start.24
  428.4 5.7 collective-permute-start.29
  442.1 5.2 collective-permute-start.32
  445.4 5.1 collective-permute-start.33
  452.4 5.4 collective-permute-start.35
  474.6 5.7 collective-permute-start.37
  480.3 7.0 collective-permute-start.38
  495.7 5.1 collective-permute-start.41
  504.6 5.4 collective-permute-start.43
  535.9 5.7 collective-permute-start.45
  558.5 5.4 collective-permute-start.50
  562.5 5.2 collective-permute-start.51
  727.8 5.7 collective-permute-start.53
  739.9 5.2 collective-permute-start.56
  852.7 5.7 collective-permute-start.61
  866.6 6.4 collective-permute-start.64
  876.9 5.4 collective-permute-start.67
  (120 other events, 1743.3 us)
where the time goes:
time: 969 us; the launch traced here: 962 us
  blocking collectives  467 us (48%)
  matrix products  169 us (17%)
  starting transfers between devices  168 us (17%)
  waiting for transfers between devices  108 us (11%)
  other arithmetic  17.4 us (2%)
  local copies, waits for them, and re-layouts  16.3 us (2%)
  between operations  13.8 us (1%)
    psum x2, blocking collectives, body(): step_size = resid_dot / lax.psum(jnp.sum(direction * curved), ('gx', 'gy'))  136 us
    psum x2, blocking collectives, body(): resid_dot = lax.psum(local_dot, ('gx', 'gy'))  135 us
    psum x2, blocking collectives, body(): fresh = lax.psum(jnp.sum(cg_resid * scaled), ('gx', 'gy'))  126 us
    ppermute x36, starting transfers between devices, passed_along(): lax.ppermute(value, axis, [(source, source + steps) for source in range(f...  89.4 us
    psum x1, blocking collectives, body(): costs_list.append(lax.psum(cost_local, ('gx', 'gy')))  69.6 us
    dot_general x36, matrix products, scatter_points(): jnp.einsum('tmo,tpo->tmp', values, one_hot_table(indices, point_count), p...  62.5 us
    ppermute x16, waiting for transfers between devices, with_halo(): after = lax.ppermute(first, axis, down)  54.3 us
    ppermute x36, waiting for transfers between devices, passed_along(): lax.ppermute(value, axis, [(source, source + steps) for source in range(f...  53.3 us
  transfers between devices with their start and end apart: 68, of which 36 were waited for; matrix products, arithmetic and copies ran while one was open for 1% of the time, Pallas kernels for 0%

commit v1 on v0

v1 whole, which is shorter than its diff:
```python
import jax
import jax.numpy as jnp
from jax import lax
from jax.experimental import pallas as pl
from jax.experimental.pallas import tpu as pltpu
from jax.sharding import PartitionSpec as P

MESH = pl.DeviceIdType.MESH
CPAR = 9
NBLK = 16
LANES = 128
TILES = 128
SLOTS = 9 * NBLK
GX = 8
GY = 16
STEPS = (1, 2, 4, 8, 16, 32, 64)
LAMBDAS = (1.0, 0.25)
PAIRS = ((0, 0), (0, 1), (0, 2), (1, 1), (1, 2), (2, 2))
OTHERS = (0, 1, 2, 3, 5, 6, 7, 8)
F32 = jnp.float32
BF16 = jnp.bfloat16
GATHER = lax.GatherDimensionNumbers(
    offset_dims=(),
    collapsed_slice_dims=(1,),
    start_index_map=(1,),
    operand_batching_dims=(0,),
    start_indices_batching_dims=(0,),
)


def pick(x, idx):
    return lax.gather(
        x, idx[:, :, None], GATHER, (1, 1), mode=lax.GatherScatterMode.PROMISE_IN_BOUNDS
    )


def lane_ids(rows):
    return lax.broadcasted_iota(jnp.int32, (rows, LANES), 1)


def sort_lanes(key):
    lane = lane_ids(key.shape[0])
    size = 2
    while size <= LANES:
        gap = size // 2
        while gap >= 1:
            other = pick(key, lane ^ gap)
            keep_low = ((lane & gap) == 0) == ((lane & size) == 0)
            key = jnp.where(keep_low, jnp.minimum(key, other), jnp.maximum(key, other))
            gap //= 2
        size *= 2
    return key


def last_at_most(seg, target):
    count = jnp.zeros_like(target)
    for step in (64, 32, 16, 8, 4, 2, 1):
        count = jnp.where(pick(seg, count + (step - 1)) <= target, count + step, count)
    return jnp.where(pick(seg, count) <= target, count + 1, count)


def column(row):
    return jnp.swapaxes(jnp.broadcast_to(row.astype(F32), (LANES, LANES)), 0, 1)


def invert(hess, damping):
    h00 = hess[0] + damping * (hess[0] + 1.0)
    h01, h02 = hess[1], hess[2]
    h11 = hess[3] + damping * (hess[3] + 1.0)
    h12 = hess[4]
    h22 = hess[5] + damping * (hess[5] + 1.0)
    c00 = h11 * h22 - h12 * h12
    c01 = h02 * h12 - h01 * h22
    c02 = h01 * h12 - h02 * h11
    c11 = h00 * h22 - h02 * h02
    c12 = h01 * h02 - h00 * h12
    c22 = h00 * h11 - h01 * h01
    det = h00 * c00 + h01 * c01 + h02 * c02
    return [c / det for c in (c00, c01, c02, c11, c12, c22)]


def apply_inverse(inv, y):
    return [
        inv[0] * y[0] + inv[1] * y[1] + inv[2] * y[2],
        inv[1] * y[0] + inv[3] * y[1] + inv[4] * y[2],
        inv[2] * y[0] + inv[4] * y[1] + inv[5] * y[2],
    ]


def lane_sum(x):
    while x.ndim > 2:
        x = jnp.sum(x, axis=0)
    return jnp.sum(x, axis=0, keepdims=True)


def kernel(
    slot_s,
    jc_h,
    jp_h,
    rs_h,
    obs_cam,
    obs_pt,
    count_r,
    tcam_r,
    tpts_r,
    start_r,
    upd_o,
    step_o,
    res_o,
    cost_o,
    jc,
    jp,
    rs,
    perm,
    endi,
    smask,
    hit_p,
    hit_c,
    pair_m,
    idx_c,
    onehot,
    zbuf,
    table,
    gg,
    bk,
    mv,
    contrib,
    recv_c,
    wsrc,
    recv_s,
    wsrc4,
    recv_s4,
    comb,
    hess_b,
    inv_b,
    ybuf,
    wbuf,
    camvec,
    camacc,
    ar_src,
    ar_mid,
    arx,
    ary,
    in_sem,
    cs_sem,
    cr_sem,
    ss_sem,
    sr_sem,
    s4s_sem,
    s4r_sem,
    axs_sem,
    axr_sem,
    ays_sem,
    ayr_sem,
):
    me_x = lax.axis_index("gx")
    me_y = lax.axis_index("gy")

    def at(dx, dy):
        return (lax.rem(me_x + (dx + GX), GX), lax.rem(me_y + (dy + GY), GY))

    barrier = pltpu.get_barrier_semaphore()
    peers = [(d, 0) for d in range(1, GX)] + [(0, d) for d in range(1, GY)]
    peers += [(-1, -1), (-1, 1), (1, -1), (1, 1)]
    for dx, dy in peers:
        pl.semaphore_signal(barrier, inc=1, device_id=at(dx, dy), device_id_type=MESH)

    copies = [
        pltpu.make_async_copy(rs_h.at[:, 0, :], rs.at[0], in_sem.at[0]),
        pltpu.make_async_copy(rs_h.at[:, 1, :], rs.at[1], in_sem.at[1]),
        pltpu.make_async_copy(jp_h, jp, in_sem.at[2]),
        pltpu.make_async_copy(jc_h, jc, in_sem.at[3]),
    ]
    for copy in copies:
        copy.start()

    lane = lane_ids(TILES)
    tcam = column(tcam_r[...]).astype(jnp.int32)
    parity = tcam & 1
    pair = tcam >> 1
    pair_m[...] = pair
    idx_c[...] = parity * 64 + obs_cam[...]
    for kind in range(2):
        ids = obs_pt[...] if kind == 0 else obs_cam[...]
        key = sort_lanes(ids * LANES + lane)
        perm[kind] = key & (LANES - 1)
        seg = key >> 7
        for i, d in enumerate(STEPS):
            same = (pltpu.roll(seg, d, axis=1) == seg) & (lane >= d)
            smask[kind, i] = jnp.where(same, 1.0, 0.0)
        target = lane if kind == 0 else lane & 63
        count = last_at_most(seg, target)
        last = jnp.maximum(count - 1, 0)
        endi[kind] = last
        found = (count > 0) & (pick(seg, last) == target)
        if kind == 0:
            hit_p[...] = jnp.where(found, 1.0, 0.0)
        else:
            here = found & ((lane >> 6) == parity)
            hit_c[0] = jnp.where(here & (pair == 0), 1.0, 0.0)
            hit_c[1] = jnp.where(here & (pair == 1), 1.0, 0.0)
    slot_row = lax.broadcasted_iota(jnp.int32, (SLOTS, TILES), 0)
    hot = jnp.where(slot_row == tpts_r[...], 1.0, 0.0).astype(BF16)
    for i in range(3):
        onehot[:, i * TILES : (i + 1) * TILES] = hot

    def summed(x, kind):
        x = pick(x, perm[kind])
        for i, d in enumerate(STEPS):
            x = x + pltpu.roll(x, d, axis=1) * smask[kind, i]
        return pick(x, endi[kind])

    def put_points(values, first):
        sums = jnp.concatenate([summed(v, 0) * hit_p[...] for v in values], axis=1)
        high = sums.astype(BF16)
        rest = sums - high.astype(F32)
        mid = rest.astype(BF16)
        low = (rest - mid.astype(F32)).astype(BF16)
        parts = jnp.concatenate([high, mid, low], axis=0)
        out = jnp.dot(onehot[...], parts, preferred_element_type=F32)
        for n in range(9):
            for m in range(3):
                contrib[n, first + m] = out[
                    n * NBLK : (n + 1) * NBLK, m * LANES : (m + 1) * LANES
                ]

    def put_cams(value_at):
        def one(group, carry):
            for j in range(3):
                k = group * 3 + j
                sums = summed(value_at(k), 1)
                top = lane_sum(sums * hit_c[0])
                bottom = lane_sum(sums * hit_c[1])
                camacc[k] = jnp.concatenate([top, bottom], axis=0)
            return carry

        lax.fori_loop(0, 3, one, 0)
        return camacc[...]

    def take_cams(vector, b):
        camvec[...] = vector
        rows = 32

        def one(chunk, carry):
            where = pl.ds(pl.multiple_of(chunk * rows, rows), rows)
            idx = idx_c[where, :]
            second = pair_m[where, :] == 1
            e0 = jnp.zeros((rows, LANES), F32)
            e1 = jnp.zeros((rows, LANES), F32)
            for k in range(CPAR):
                v = camvec[k]
                src = jnp.where(
                    second,
                    jnp.broadcast_to(v[1:2], (rows, LANES)),
                    jnp.broadcast_to(v[0:1], (rows, LANES)),
                )
                got = pick(src, idx)
                e0 = e0 + jc[k, where, :] * got
                e1 = e1 + jc[CPAR + k, where, :] * got
            gg[b, 0, where, :] = e0
            gg[b, 1, where, :] = e1
            return carry

        lax.fori_loop(0, TILES // rows, one, 0)

    def to_points(e0, e1):
        return [jp[m] * e0 + jp[3 + m] * e1 for m in range(3)]

    def collect_start(comps):
        for r, n in enumerate(OTHERS):
            a, b = divmod(n, 3)
            pltpu.make_async_remote_copy(
                src_ref=contrib.at[n, pl.ds(0, comps)],
                dst_ref=recv_c.at[r, pl.ds(0, comps)],
                send_sem=cs_sem.at[r],
                recv_sem=cr_sem.at[r],
                device_id=at(a - 1, b - 1),
                device_id_type=MESH,
            ).start()

    def collect_wait(comps):
        for r, n in enumerate(OTHERS):
            pltpu.make_async_copy(
                contrib.at[n, pl.ds(0, comps)], recv_c.at[r, pl.ds(0, comps)], cr_sem.at[r]
            ).wait()
        for r, n in enumerate(OTHERS):
            pltpu.make_async_copy(
                contrib.at[n, pl.ds(0, comps)], recv_c.at[r, pl.ds(0, comps)], cs_sem.at[r]
            ).wait()
        total = []
        for m in range(comps):
            s = contrib[4, m]
            for r in range(8):
                s = s + recv_c[r, m]
            total.append(s)
        return total

    def spread_start(values, src, dst, send_sem, recv_sem):
        for m, v in enumerate(values):
            src[m] = v
            dst[4, m] = v
        for r, n in enumerate(OTHERS):
            a, b = divmod(n, 3)
            pltpu.make_async_remote_copy(
                src_ref=src,
                dst_ref=dst.at[8 - n],
                send_sem=send_sem.at[r],
                recv_sem=recv_sem.at[r],
                device_id=at(a - 1, b - 1),
                device_id_type=MESH,
            ).start()

    def spread_wait(src, dst, send_sem, recv_sem):
        for r, n in enumerate(OTHERS):
            pltpu.make_async_copy(src, dst.at[8 - n], recv_sem.at[r]).wait()
        for r, n in enumerate(OTHERS):
            pltpu.make_async_copy(src, dst.at[8 - n], send_sem.at[r]).wait()

    def take_points(src):
        def one(chunk, carry):
            for i in range(8):
                t = chunk * 8 + i
                slot = slot_s[t]
                n = slot >> 4
                q = slot & 15
                for m in range(3):
                    table[m, pl.ds(t, 1), :] = src[n, m, pl.ds(q, 1), :]
            return carry

        lax.fori_loop(0, TILES // 8, one, 0)
        return [pick(table[m], obs_pt[...]) for m in range(3)]

    def eliminate(e0, e1, b, src):
        near = take_points(src)
        bk[b, 0] = e0 - (jp[0] * near[0] + jp[1] * near[1] + jp[2] * near[2])
        bk[b, 1] = e1 - (jp[3] * near[0] + jp[4] * near[1] + jp[5] * near[2])
        return put_cams(lambda k: jc[k] * bk[b, 0] + jc[CPAR + k] * bk[b, 1])

    def reduce_x_start(a, rows):
        ar_src[a] = jnp.concatenate(rows + [jnp.zeros((8 - len(rows), LANES), F32)], axis=0)
        arx[a, me_x] = ar_src[a]
        for d in range(1, GX):
            pltpu.make_async_remote_copy(
                src_ref=ar_src.at[a],
                dst_ref=arx.at[a, me_x],
                send_sem=axs_sem.at[a, d],
                recv_sem=axr_sem.at[a, d],
                device_id=at(d, 0),
                device_id_type=MESH,
            ).start()

    def reduce_y_start(a):
        for d in range(1, GX):
            pltpu.make_async_copy(ar_src.at[a], arx.at[a, 0], axr_sem.at[a, d]).wait()
        ar_mid[a] = jnp.sum(arx[a], axis=0)
        ary[a, me_y] = ar_mid[a]
        for d in range(1, GY):
            pltpu.make_async_remote_copy(
                src_ref=ar_mid.at[a],
                dst_ref=ary.at[a, me_y],
                send_sem=ays_sem.at[a, d],
                recv_sem=ayr_sem.at[a, d],
                device_id=at(0, d),
                device_id_type=MESH,
            ).start()

    def reduce_wait(a):
        for d in range(1, GY):
            pltpu.make_async_copy(ar_mid.at[a], ary.at[a, 0], ayr_sem.at[a, d]).wait()
        total = jnp.sum(jnp.sum(ary[a], axis=0), axis=1, keepdims=True)
        wide = jnp.broadcast_to(total, (8, LANES))
        return [wide[i : i + 1] for i in range(8)]

    def reduce_drain(a):
        for d in range(1, GX):
            pltpu.make_async_copy(ar_src.at[a], arx.at[a, 0], axs_sem.at[a, d]).wait()
        for d in range(1, GY):
            pltpu.make_async_copy(ar_mid.at[a], ary.at[a, 0], ays_sem.at[a, d]).wait()

    valid = jnp.where(lane < column(count_r[...]).astype(jnp.int32), 1.0, 0.0)
    for copy in copies:
        copy.wait()
    for k in range(2):
        rs[k] = rs[k] * valid
    for k in range(6):
        jp[k] = jp[k] * valid
    for k in range(18):
        jc[k] = jc[k] * valid

    start = start_r[...]
    take_cams(start, 0)

    for c, (i, j) in enumerate(PAIRS):
        zbuf[c] = jp[i] * jp[j] + jp[3 + i] * jp[3 + j]
    for m, v in enumerate(to_points(rs[0], rs[1])):
        zbuf[6 + m] = v
    for m, v in enumerate(to_points(gg[0, 0], gg[0, 1])):
        zbuf[9 + m] = v

    def first_points(group, carry):
        put_points([zbuf[group * 3 + m] for m in range(3)], group * 3)
        return carry

    lax.fori_loop(0, 4, first_points, 0)
    pl.semaphore_wait(barrier, len(peers))
    collect_start(12)
    diag = put_cams(lambda k: jc[k] * jc[k] + jc[CPAR + k] * jc[CPAR + k])
    cost_row = lane_sum(rs[...] * rs[...])
    owned = collect_wait(12)
    for c in range(6):
        hess_b[c] = owned[c]
    y_start = owned[9:12]
    ybuf[0] = jnp.stack([owned[6 + m] + owned[9 + m] for m in range(3)])

    update = start
    upd_sum = jnp.zeros_like(start)
    step_sum = jnp.zeros((3, NBLK, LANES), F32)
    for k in range(2):
        mv[k] = rs[k] + gg[0, k]

    for step in range(2):
        damping = LAMBDAS[step]
        last = step == 1
        cam_damp = damping * (diag + 1.0)
        precond = diag + cam_damp
        if step == 0:
            inv = invert([hess_b[c] for c in range(6)], damping)
            for c in range(6):
                inv_b[c] = inv[c]
            w0 = apply_inverse(inv, [ybuf[0, m] for m in range(3)])
            wbuf[0] = jnp.stack(w0)
            spread_start(w0, wsrc, recv_s, ss_sem, sr_sem)
            spread_wait(wsrc, recv_s, ss_sem, sr_sem)
            sums = eliminate(mv[0], mv[1], 0, recv_s)
        else:
            sums = eliminate(mv[0], mv[1], 0, comb)
        r0 = -sums - cam_damp * update
        z0 = r0 / precond

        def operator(vector, b):
            take_cams(vector, b)
            put_points(to_points(gg[b, 0], gg[b, 1]), 0)
            collect_start(3)

        def operator_finish(vector, b):
            y = collect_wait(3)
            ybuf[b] = jnp.stack(y)
            w = apply_inverse([inv_b[c] for c in range(6)], y)
            wbuf[b] = jnp.stack(w)
            spread_start(w, wsrc, recv_s, ss_sem, sr_sem)

        def operator_end(vector, b):
            spread_wait(wsrc, recv_s, ss_sem, sr_sem)
            return eliminate(gg[b, 0], gg[b, 1], b, recv_s) + cam_damp * vector

        operator(z0, 1)
        operator_finish(z0, 1)
        c0 = operator_end(z0, 1)
        u = c0 / precond
        first = 2 * step
        reduce_x_start(
            first, [lane_sum(r0 * z0), lane_sum(z0 * c0), lane_sum(c0 * u), cost_row]
        )
        operator(u, 2)
        reduce_y_start(first)
        operator_finish(u, 2)
        q = operator_end(u, 2)
        dots = reduce_wait(first)
        resid_dot, curve, square = dots[0], dots[1], dots[2]
        cost_o[pl.ds(step, 1), :] = 0.5 * dots[3]
        alpha = resid_dot / curve
        beta = (resid_dot - 2.0 * alpha * curve + alpha * alpha * square) / resid_dot
        r1 = r0 - alpha * c0
        z1 = r1 / precond
        d1 = z1 + beta * z0
        sd1 = (1.0 + beta) * c0 - alpha * q
        rows = [lane_sum(r1 * z1), lane_sum(d1 * sd1)]
        if last:
            near = bk[0] + alpha * bk[1]
            turn = (1.0 + beta) * bk[1] - alpha * bk[2]
            rows += [lane_sum(near * near), lane_sum(near * turn), lane_sum(turn * turn)]
        second = first + 1
        reduce_x_start(second, rows)
        if not last:
            hess = [hess_b[c] for c in range(6)]
            inv = invert(hess, LAMBDAS[1])
            for c in range(6):
                inv_b[c] = inv[c]
            scale = [damping * (hess[c] + 1.0) for c in (0, 3, 5)]
            held = []
            for b in range(3):
                held.append([scale[m] * wbuf[b, m] + ybuf[b, m] for m in range(3)])
            base = [
                scale[m] * wbuf[0, m] + y_start[m] + alpha * held[1][m] for m in range(3)
            ]
            move = [(1.0 + beta) * held[1][m] - alpha * held[2][m] for m in range(3)]
            spread_start(apply_inverse(inv, base) + apply_inverse(inv, move), wsrc4, recv_s4, s4s_sem, s4r_sem)
        reduce_y_start(second)
        if not last:
            spread_wait(wsrc4, recv_s4, s4s_sem, s4r_sem)
        dots = reduce_wait(second)
        alpha1 = dots[0] / dots[1]
        ca = alpha + alpha1 * (1.0 + beta)
        cb = -(alpha1 * alpha)
        update = update + alpha * z0 + alpha1 * d1
        upd_sum = upd_sum + update
        step_sum = step_sum - (wbuf[0] + ca * wbuf[1] + cb * wbuf[2])
        if not last:
            for r in range(2):
                res = bk[0, r] + ca * bk[1, r] + cb * bk[2, r]
                rs[r] = res
                mv[r] = res + (gg[0, r] + ca * gg[1, r] + cb * gg[2, r])
            cost_row = lane_sum(rs[...] * rs[...])
            for n in range(9):
                for m in range(3):
                    comb[n, m] = recv_s4[n, m] + alpha1 * recv_s4[n, 3 + m]
            wbuf[0] = wsrc4[0:3] + alpha1 * wsrc4[3:6]
        else:
            for r in range(2):
                res_o[r] = bk[0, r] + ca * bk[1, r] + cb * bk[2, r]
            cost_o[pl.ds(2, 1), :] = 0.5 * (
                dots[2] + 2.0 * alpha1 * dots[3] + alpha1 * alpha1 * dots[4]
            )
    upd_o[...] = upd_sum
    step_o[...] = step_sum
    cost_o[pl.ds(3, 5), :] = jnp.zeros((5, LANES), F32)
    for a in range(4):
        reduce_drain(a)


def body(
    jac_cam,
    jac_pt,
    resid0,
    obs_count,
    tile_camera,
    tile_points,
    obs_camera,
    obs_point,
    cam_params,
    pt_params,
    cg_start,
):
    start = jnp.transpose(
        cg_start[0, 0].reshape(2, 2, CPAR, 64), (2, 0, 1, 3)
    ).reshape(CPAR, 2, LANES)
    vmem = pl.BlockSpec(memory_space=pltpu.VMEM)
    hbm = pl.BlockSpec(memory_space=pl.ANY)
    big = (TILES, LANES)
    blk = (NBLK, LANES)
    dma = pltpu.SemaphoreType.DMA
    upd, steps, res, costs = pl.pallas_call(
        kernel,
        out_shape=[
            jax.ShapeDtypeStruct((CPAR, 2, LANES), F32),
            jax.ShapeDtypeStruct((3,) + blk, F32),
            jax.ShapeDtypeStruct((2,) + big, F32),
            jax.ShapeDtypeStruct((8, LANES), F32),
        ],
        in_specs=[pl.BlockSpec(memory_space=pltpu.SMEM)] + [hbm] * 3 + [vmem] * 6,
        out_specs=[vmem] * 4,
        scratch_shapes=[
            pltpu.VMEM((18,) + big, F32),
            pltpu.VMEM((6,) + big, F32),
            pltpu.VMEM((2,) + big, F32),
            pltpu.VMEM((2,) + big, jnp.int32),
            pltpu.VMEM((2,) + big, jnp.int32),
            pltpu.VMEM((2, 7) + big, F32),
            pltpu.VMEM(big, F32),
            pltpu.VMEM((2,) + big, F32),
            pltpu.VMEM(big, jnp.int32),
            pltpu.VMEM(big, jnp.int32),
            pltpu.VMEM((SLOTS, 3 * TILES), BF16),
            pltpu.VMEM((12,) + big, F32),
            pltpu.VMEM((3,) + big, F32),
            pltpu.VMEM((3, 2) + big, F32),
            pltpu.VMEM((3, 2) + big, F32),
            pltpu.VMEM((2,) + big, F32),
            pltpu.VMEM((9, 12) + blk, F32),
            pltpu.VMEM((8, 12) + blk, F32),
            pltpu.VMEM((3,) + blk, F32),
            pltpu.VMEM((9, 3) + blk, F32),
            pltpu.VMEM((6,) + blk, F32),
            pltpu.VMEM((9, 6) + blk, F32),
            pltpu.VMEM((9, 3) + blk, F32),
            pltpu.VMEM((6,) + blk, F32),
            pltpu.VMEM((6,) + blk, F32),
            pltpu.VMEM((3, 3) + blk, F32),
            pltpu.VMEM((3, 3) + blk, F32),
            pltpu.VMEM((CPAR, 2, LANES), F32),
            pltpu.VMEM((CPAR, 2, LANES), F32),
            pltpu.VMEM((4, 8, LANES), F32),
            pltpu.VMEM((4, 8, LANES), F32),
            pltpu.VMEM((4, GX, 8, LANES), F32),
            pltpu.VMEM((4, GY, 8, LANES), F32),
            dma((4,)),
            dma((8,)),
            dma((8,)),
            dma((8,)),
            dma((8,)),
            dma((8,)),
            dma((8,)),
            dma((4, GX)),
            dma((4, GX)),
            dma((4, GY)),
            dma((4, GY)),
        ],
        compiler_params=pltpu.CompilerParams(
            collective_id=0, has_side_effects=True, vmem_limit_bytes=48 * 1024 * 1024
        ),
    )(
        tile_points[0, 0],
        jnp.transpose(jac_cam[0, 0], (1, 0, 2)),
        jnp.transpose(jac_pt[0, 0], (1, 0, 2)),
        resid0[0, 0],
        obs_camera[0, 0],
        obs_point[0, 0],
        obs_count[0],
        tile_camera[0],
        tile_points[0],
        start,
    )
    moved = jnp.transpose(upd.reshape(CPAR, 2, 2, 64), (1, 2, 0, 3)).reshape(4, CPAR, 64)
    cam_out = cam_params + moved[None, None]
    pt_out = pt_params + jnp.transpose(steps, (1, 0, 2))[None, None]
    res_out = jnp.transpose(res, (1, 0, 2))[None, None]
    return cam_out, pt_out, res_out, costs[:3, 0]


def solution(mesh):
    wide = P("gx", "gy", None, None, None)
    in_specs = (
        wide,
        wide,
        wide,
        P("gx", "gy", None),
        P("gx", "gy", None),
        P("gx", "gy", None),
        P("gx", "gy", None, None),
        P("gx", "gy", None, None),
        wide,
        wide,
        wide,
    )
    out_specs = (wide, wide, wide, P())
    return jax.shard_map(body, mesh=mesh, in_specs=in_specs, out_specs=out_specs, check_vma=False)
```

time: 969 us -> 127 us (0.13)
  blocking collectives: 467 us -> 0 us
  matrix products: 169 us -> 0 us
  starting transfers between devices: 168 us -> 0 us
  Pallas kernels: 0 us -> 116 us
  waiting for transfers between devices: 108 us -> 0 us
  other arithmetic: 17.4 us -> 1.22 us
  between operations: 13.8 us -> 0.67 us
    psum x7 -> x0, blocking collectives: 467 us -> none  [the longest x2 136 us: body(): step_size = resid_dot / lax.psum(jnp.sum(direction * curved), ('gx', 'gy'))]
    dot_general x155 -> x0, matrix products: 169 us -> none  [the longest x36 62.5 us: scatter_points(): jnp.einsum('tmo,tpo->tmp', values, one_hot_table(indices, point_count), p...]
    ppermute x68 -> x0, starting transfers between devices: 168 us -> none  [the longest x36 89.4 us: passed_along(): lax.ppermute(value, axis, [(source, source + steps) for source in range(f...]
    pallas_call x0 -> x1, Pallas kernels: none -> 116 us  [body(): pl.pallas_call(kernel, out_shape=[jax.ShapeDtypeStruct((CPAR, 2, LANES),...]
    ppermute x68 -> x0, waiting for transfers between devices: 108 us -> none  [the longest x16 54.3 us: with_halo(): after = lax.ppermute(first, axis, down)]
  transfers between devices with their start and end apart: 68 -> 0, of which waited for: 36 -> 0; matrix products, arithmetic and copies ran while one was open for 1% -> 0% of each run, Pallas kernels for 0% -> 0%
where the time goes in v1:
time: 127 us
  Pallas kernels  116 us (91%)
  local copies, waits for them, and re-layouts  9.11 us (7%)
    pallas_call x1, Pallas kernels, body(): pl.pallas_call(kernel, out_shape=[jax.ShapeDtypeStruct((CPAR, 2, LANES),...  116 us
    unnamed x21, local copies, waits for them, and re-layouts  7.57 us

profile of v1, /device:TPU:1, one launch (start us, length us, event | category | flops | bytes accessed | tf_op | source)
XLA Modules:
  0.0 126.6 jit_solution(15951787227950219904)
XLA Ops:
  0.6 0.0 copy-start.9
  0.6 0.0 copy-start.8
  0.7 0.8 reshape.14.start_r
  1.5 0.0 copy-start
  1.5 1.3 copy-done
  2.7 0.0 copy-start.1
  2.7 1.0 copy-done.1
  3.7 0.0 copy-start.2
  3.7 0.9 copy-done.2
  4.6 0.0 copy-start.3
  4.6 0.8 copy-done.3
  5.5 0.0 copy-start.4
  5.5 0.8 copy-done.4
  6.3 0.0 copy-start.5
  6.3 0.7 copy-done.5
  7.0 0.0 copy-start.6
  7.0 0.7 copy-done.6
  7.6 0.0 copy-start.7
  7.6 0.7 copy-done.7
  8.3 115.6 %shard_map.138 = (f32[9,2,128]{2,1,0:T(2,128)S(1)}, f32[3,16,128]{2,1,0:T(8,128)S(1)}, f32[2,128,128]{2,1,0:T(8,128)S(1)}, f32[8,128]{1,0:T(8,128)S(1)}) custom-call(s32[128]{0:T(128)S(1)} %bitcast.32, f32[18,128,128]{2,1,0:T(8,128)S(1)} %bitcast.26, f32[6,128,128]{2,1,0:T(8,128)S(1)} %bitcast.27, f32[128,2,128]{2,1,0:T(2,128)S(1)} %bitcast.29, ...), custom_call_target="tpu_custom_call" | custom-call | tf_op jit(solution)/shard_map/pallas_call | solution.py:552
  123.9 0.8 copy.16
  124.7 0.1 reshape.15
  124.8 0.0 copy-done.9
  124.8 0.6 add.6
  125.4 0.0 copy-done.8
  125.4 0.6 bitcast_add_fusion
  126.0 0.6 slice_reduce_fusion
Async XLA Ops:
  0.6 124.2 %copy-start.9 = (f32[1,1,4,9,64]{4,2,3,1,0:T(4,128)S(1)}, f32[1,1,4,9,64]{4,2,3,1,0:T(4,128)}, u32[]{:S(2)}) copy-start(f32[1,1,4,9,64]{4,2,3,1,0:T(4,128)} %param.19) | copy-start | bytes 27652
  0.6 124.8 %copy-start.8 = (f32[1,1,16,3,128]{4,2,3,1,0:T(8,128)S(1)}, f32[1,1,16,3,128]{4,2,3,1,0:T(8,128)}, u32[]{:S(2)}) copy-start(f32[1,1,16,3,128]{4,2,3,1,0:T(8,128)} %param.20) | copy-start | bytes 73732
  1.5 1.3 %copy-start = (f32[1,1,128,18,128]{4,2,3,1,0:T(8,128)S(1)}, f32[1,1,128,18,128]{4,2,3,1,0:T(8,128)}, u32[]{:S(2)}) copy-start(f32[1,1,128,18,128]{4,2,3,1,0:T(8,128)} %param.11) | copy-start | bytes 3538948
  2.7 1.0 copy-start.1
  3.7 0.9 copy-start.2
  4.6 0.8 copy-start.3
  5.5 0.8 copy-start.4
  6.3 0.7 copy-start.5
  7.0 0.7 copy-start.6
  7.6 0.7 copy-start.7

commit v2 on v1

--- a/solution.py
+++ b/solution.py
@@ -17,6 +17,7 @@
 LAMBDAS = (1.0, 0.25)
 PAIRS = ((0, 0), (0, 1), (0, 2), (1, 1), (1, 2), (2, 2))
 OTHERS = (0, 1, 2, 3, 5, 6, 7, 8)
+ORDER = tuple((OTHERS.index(n), n) for n in (0, 2, 6, 8, 3, 5, 1, 7))
 F32 = jnp.float32
 BF16 = jnp.bfloat16
 GATHER = lax.GatherDimensionNumbers(
@@ -128,9 +129,8 @@
     recv_c,
     wsrc,
     recv_s,
-    wsrc4,
-    recv_s4,
-    comb,
+    wsrc_w,
+    recv_w,
     hess_b,
     inv_b,
     ybuf,
@@ -138,20 +138,16 @@
     camvec,
     camacc,
     ar_src,
-    ar_mid,
     arx,
-    ary,
     in_sem,
     cs_sem,
     cr_sem,
     ss_sem,
     sr_sem,
-    s4s_sem,
-    s4r_sem,
-    axs_sem,
-    axr_sem,
-    ays_sem,
-    ayr_sem,
+    ws_sem,
+    wr_sem,
+    as_sem,
+    ar_sem,
 ):
     me_x = lax.axis_index("gx")
     me_y = lax.axis_index("gy")
@@ -159,11 +155,38 @@
     def at(dx, dy):
         return (lax.rem(me_x + (dx + GX), GX), lax.rem(me_y + (dy + GY), GY))
 
+    me = me_x * GY + me_y
+    here = {}
+    for n in OTHERS:
+        a, b = divmod(n, 3)
+        x, y = me_x + (a - 1), me_y + (b - 1)
+        here[n] = (x >= 0) & (x < GX) & (y >= 0) & (y < GY)
+
+    def to_all(act):
+        def row(j, carry):
+            dy = lax.rem(j + 5, GY - 1) + 1
+            for dx in (4, 3, 5, 2, 6, 1, 7, 0):
+                act(dx, dy)
+            return carry
+
+        lax.fori_loop(0, GY - 1, row, 0)
+        for dx in (4, 3, 5, 2, 6, 1, 7):
+            act(dx, 0)
+
+    for r, n in enumerate(OTHERS):
+
+        @pl.when(jnp.logical_not(here[n]))
+        def _(r=r, n=n):
+            recv_c[r] = jnp.zeros_like(recv_c[r])
+            recv_s[n] = jnp.zeros_like(recv_s[n])
+            recv_w[n] = jnp.zeros_like(recv_w[n])
+
     barrier = pltpu.get_barrier_semaphore()
-    peers = [(d, 0) for d in range(1, GX)] + [(0, d) for d in range(1, GY)]
-    peers += [(-1, -1), (-1, 1), (1, -1), (1, 1)]
-    for dx, dy in peers:
-        pl.semaphore_signal(barrier, inc=1, device_id=at(dx, dy), device_id_type=MESH)
+    to_all(
+        lambda dx, dy: pl.semaphore_signal(
+            barrier, inc=1, device_id=at(dx, dy), device_id_type=MESH
+        )
+    )
 
     copies = [
         pltpu.make_async_copy(rs_h.at[:, 0, :], rs.at[0], in_sem.at[0]),
@@ -180,7 +203,8 @@
     pair = tcam >> 1
     pair_m[...] = pair
     idx_c[...] = parity * 64 + obs_cam[...]
-    for kind in range(2):
+
+    def order(kind):
         ids = obs_pt[...] if kind == 0 else obs_cam[...]
         key = sort_lanes(ids * LANES + lane)
         perm[kind] = key & (LANES - 1)
@@ -196,9 +220,11 @@
         if kind == 0:
             hit_p[...] = jnp.where(found, 1.0, 0.0)
         else:
-            here = found & ((lane >> 6) == parity)
-            hit_c[0] = jnp.where(here & (pair == 0), 1.0, 0.0)
-            hit_c[1] = jnp.where(here & (pair == 1), 1.0, 0.0)
+            mine = found & ((lane >> 6) == parity)
+            hit_c[0] = jnp.where(mine & (pair == 0), 1.0, 0.0)
+            hit_c[1] = jnp.where(mine & (pair == 1), 1.0, 0.0)
+
+    order(0)
     slot_row = lax.broadcasted_iota(jnp.int32, (SLOTS, TILES), 0)
     hot = jnp.where(slot_row == tpts_r[...], 1.0, 0.0).astype(BF16)
     for i in range(3):
@@ -267,26 +293,30 @@
         return [jp[m] * e0 + jp[3 + m] * e1 for m in range(3)]
 
     def collect_start(comps):
-        for r, n in enumerate(OTHERS):
+        for r, n in ORDER:
             a, b = divmod(n, 3)
-            pltpu.make_async_remote_copy(
-                src_ref=contrib.at[n, pl.ds(0, comps)],
-                dst_ref=recv_c.at[r, pl.ds(0, comps)],
-                send_sem=cs_sem.at[r],
-                recv_sem=cr_sem.at[r],
-                device_id=at(a - 1, b - 1),
-                device_id_type=MESH,
-            ).start()
+
+            @pl.when(here[n])
+            def _(r=r, n=n, a=a, b=b):
+                pltpu.make_async_remote_copy(
+                    src_ref=contrib.at[n, pl.ds(0, comps)],
+                    dst_ref=recv_c.at[r, pl.ds(0, comps)],
+                    send_sem=cs_sem.at[r],
+                    recv_sem=cr_sem.at[r],
+                    device_id=at(a - 1, b - 1),
+                    device_id_type=MESH,
+                ).start()
 
     def collect_wait(comps):
-        for r, n in enumerate(OTHERS):
-            pltpu.make_async_copy(
-                contrib.at[n, pl.ds(0, comps)], recv_c.at[r, pl.ds(0, comps)], cr_sem.at[r]
-            ).wait()
-        for r, n in enumerate(OTHERS):
-            pltpu.make_async_copy(
-                contrib.at[n, pl.ds(0, comps)], recv_c.at[r, pl.ds(0, comps)], cs_sem.at[r]
-            ).wait()
+        for sem, flip in ((cr_sem, True), (cs_sem, False)):
+            for r, n in enumerate(OTHERS):
+
+                @pl.when(here[8 - n] if flip else here[n])
+                def _(r=r, n=n, sem=sem):
+                    pltpu.make_async_copy(
+                        contrib.at[n, pl.ds(0, comps)], recv_c.at[r, pl.ds(0, comps)], sem.at[r]
+                    ).wait()
+
         total = []
         for m in range(comps):
             s = contrib[4, m]
@@ -299,24 +329,29 @@
         for m, v in enumerate(values):
             src[m] = v
             dst[4, m] = v
-        for r, n in enumerate(OTHERS):
+        for r, n in ORDER:
             a, b = divmod(n, 3)
-            pltpu.make_async_remote_copy(
-                src_ref=src,
-                dst_ref=dst.at[8 - n],
-                send_sem=send_sem.at[r],
-                recv_sem=recv_sem.at[r],
-                device_id=at(a - 1, b - 1),
-                device_id_type=MESH,
-            ).start()
+
+            @pl.when(here[n])
+            def _(r=r, n=n, a=a, b=b):
+                pltpu.make_async_remote_copy(
+                    src_ref=src,
+                    dst_ref=dst.at[8 - n],
+                    send_sem=send_sem.at[r],
+                    recv_sem=recv_sem.at[r],
+                    device_id=at(a - 1, b - 1),
+                    device_id_type=MESH,
+                ).start()
 
     def spread_wait(src, dst, send_sem, recv_sem):
-        for r, n in enumerate(OTHERS):
-            pltpu.make_async_copy(src, dst.at[8 - n], recv_sem.at[r]).wait()
-        for r, n in enumerate(OTHERS):
-            pltpu.make_async_copy(src, dst.at[8 - n], send_sem.at[r]).wait()
-
-    def take_points(src):
+        for sem, flip in ((recv_sem, True), (send_sem, False)):
+            for r, n in enumerate(OTHERS):
+
+                @pl.when(here[8 - n] if flip else here[n])
+                def _(r=r, n=n, sem=sem):
+                    pltpu.make_async_copy(src, dst.at[8 - n], sem.at[r]).wait()
+
+    def take_points(src, first=0):
         def one(chunk, carry):
             for i in range(8):
                 t = chunk * 8 + i
@@ -324,58 +359,54 @@
                 n = slot >> 4
                 q = slot & 15
                 for m in range(3):
-                    table[m, pl.ds(t, 1), :] = src[n, m, pl.ds(q, 1), :]
+                    table[m, pl.ds(t, 1), :] = src[n, first + m, pl.ds(q, 1), :]
             return carry
 
         lax.fori_loop(0, TILES // 8, one, 0)
         return [pick(table[m], obs_pt[...]) for m in range(3)]
 
-    def eliminate(e0, e1, b, src):
-        near = take_points(src)
+    def eliminate(e0, e1, near, b):
         bk[b, 0] = e0 - (jp[0] * near[0] + jp[1] * near[1] + jp[2] * near[2])
         bk[b, 1] = e1 - (jp[3] * near[0] + jp[4] * near[1] + jp[5] * near[2])
+
+    def back_to_cams(b):
         return put_cams(lambda k: jc[k] * bk[b, 0] + jc[CPAR + k] * bk[b, 1])
 
-    def reduce_x_start(a, rows):
-        ar_src[a] = jnp.concatenate(rows + [jnp.zeros((8 - len(rows), LANES), F32)], axis=0)
-        arx[a, me_x] = ar_src[a]
-        for d in range(1, GX):
+    def total_start(a, rows):
+        held = jnp.concatenate(rows + [jnp.zeros((8 - len(rows), LANES), F32)], axis=0)
+        sums = jnp.sum(held, axis=1, keepdims=True)
+        lane8 = lane_ids(8)
+        own = lax.broadcasted_iota(jnp.int32, (8, LANES), 0)
+        row = jnp.sum(jnp.where(lane8 == own, sums, 0.0), axis=0, keepdims=True)
+        ar_src[a] = row
+        arx[a, pl.ds(me, 1), :] = row
+
+        def send(dx, dy):
             pltpu.make_async_remote_copy(
                 src_ref=ar_src.at[a],
-                dst_ref=arx.at[a, me_x],
-                send_sem=axs_sem.at[a, d],
-                recv_sem=axr_sem.at[a, d],
-                device_id=at(d, 0),
+                dst_ref=arx.at[a, pl.ds(me, 1)],
+                send_sem=as_sem.at[a],
+                recv_sem=ar_sem.at[a],
+                device_id=at(dx, dy),
                 device_id_type=MESH,
             ).start()
 
-    def reduce_y_start(a):
-        for d in range(1, GX):
-            pltpu.make_async_copy(ar_src.at[a], arx.at[a, 0], axr_sem.at[a, d]).wait()
-        ar_mid[a] = jnp.sum(arx[a], axis=0)
-        ary[a, me_y] = ar_mid[a]
-        for d in range(1, GY):
-            pltpu.make_async_remote_copy(
-                src_ref=ar_mid.at[a],
-                dst_ref=ary.at[a, me_y],
-                send_sem=ays_sem.at[a, d],
-                recv_sem=ayr_sem.at[a, d],
-                device_id=at(0, d),
-                device_id_type=MESH,
-            ).start()
-
-    def reduce_wait(a):
-        for d in range(1, GY):
-            pltpu.make_async_copy(ar_mid.at[a], ary.at[a, 0], ayr_sem.at[a, d]).wait()
-        total = jnp.sum(jnp.sum(ary[a], axis=0), axis=1, keepdims=True)
-        wide = jnp.broadcast_to(total, (8, LANES))
-        return [wide[i : i + 1] for i in range(8)]
-
-    def reduce_drain(a):
-        for d in range(1, GX):
-            pltpu.make_async_copy(ar_src.at[a], arx.at[a, 0], axs_sem.at[a, d]).wait()
-        for d in range(1, GY):
-            pltpu.make_async_copy(ar_mid.at[a], ary.at[a, 0], ays_sem.at[a, d]).wait()
+        to_all(send)
+
+    def total_wait(a):
+        pltpu.make_async_copy(
+            arx.at[a, pl.ds(0, 127)], arx.at[a, pl.ds(0, 127)], ar_sem.at[a]
+        ).wait()
+        row = jnp.sum(arx[a], axis=0, keepdims=True)
+        lane1 = lane_ids(1)
+        return [
+            jnp.sum(jnp.where(lane1 == i, row, 0.0), axis=1, keepdims=True) for i in range(8)
+        ]
+
+    def total_drain(a):
+        pltpu.make_async_copy(
+            arx.at[a, pl.ds(0, 127)], arx.at[a, pl.ds(0, 127)], as_sem.at[a]
+        ).wait()
 
     valid = jnp.where(lane < column(count_r[...]).astype(jnp.int32), 1.0, 0.0)
     for copy in copies:
@@ -402,8 +433,9 @@
         return carry
 
     lax.fori_loop(0, 4, first_points, 0)
-    pl.semaphore_wait(barrier, len(peers))
+    pl.semaphore_wait(barrier, GX * GY - 1)
     collect_start(12)
+    order(1)
     diag = put_cams(lambda k: jc[k] * jc[k] + jc[CPAR + k] * jc[CPAR + k])
     cost_row = lane_sum(rs[...] * rs[...])
     owned = collect_wait(12)
@@ -418,69 +450,100 @@
     for k in range(2):
         mv[k] = rs[k] + gg[0, k]
 
+    def weighted(w):
+        h = [hess_b[c] for c in range(6)]
+        return [
+            h[0] * w[0] + h[1] * w[1] + h[2] * w[2],
+            h[1] * w[0] + h[3] * w[1] + h[4] * w[2],
+            h[2] * w[0] + h[4] * w[1] + h[5] * w[2],
+        ]
+
+    def inner(u, v):
+        return lane_sum(u[0] * v[0] + u[1] * v[1] + u[2] * v[2])
+
+    def three(buf, b):
+        return [buf[b, m] for m in range(3)]
+
+    def mix(p, u, q, v):
+        return [p * u[m] + q * v[m] for m in range(3)]
+
+    inv = invert([hess_b[c] for c in range(6)], LAMBDAS[0])
+    for c in range(6):
+        inv_b[c] = inv[c]
+    w0 = apply_inverse(inv, three(ybuf, 0))
+    wbuf[0] = jnp.stack(w0)
+    spread_start(w0, wsrc, recv_s, ss_sem, sr_sem)
+    spread_wait(wsrc, recv_s, ss_sem, sr_sem)
+    near = take_points(recv_s)
+
     for step in range(2):
         damping = LAMBDAS[step]
         last = step == 1
         cam_damp = damping * (diag + 1.0)
         precond = diag + cam_damp
-        if step == 0:
-            inv = invert([hess_b[c] for c in range(6)], damping)
-            for c in range(6):
-                inv_b[c] = inv[c]
-            w0 = apply_inverse(inv, [ybuf[0, m] for m in range(3)])
-            wbuf[0] = jnp.stack(w0)
-            spread_start(w0, wsrc, recv_s, ss_sem, sr_sem)
-            spread_wait(wsrc, recv_s, ss_sem, sr_sem)
-            sums = eliminate(mv[0], mv[1], 0, recv_s)
-        else:
-            sums = eliminate(mv[0], mv[1], 0, comb)
-        r0 = -sums - cam_damp * update
+        eliminate(mv[0], mv[1], near, 0)
+        r0 = -back_to_cams(0) - cam_damp * update
         z0 = r0 / precond
 
-        def operator(vector, b):
-            take_cams(vector, b)
-            put_points(to_points(gg[b, 0], gg[b, 1]), 0)
-            collect_start(3)
-
-        def operator_finish(vector, b):
-            y = collect_wait(3)
-            ybuf[b] = jnp.stack(y)
-            w = apply_inverse([inv_b[c] for c in range(6)], y)
-            wbuf[b] = jnp.stack(w)
-            spread_start(w, wsrc, recv_s, ss_sem, sr_sem)
-
-        def operator_end(vector, b):
-            spread_wait(wsrc, recv_s, ss_sem, sr_sem)
-            return eliminate(gg[b, 0], gg[b, 1], b, recv_s) + cam_damp * vector
-
-        operator(z0, 1)
-        operator_finish(z0, 1)
-        c0 = operator_end(z0, 1)
+        take_cams(z0, 1)
+        put_points(to_points(gg[1, 0], gg[1, 1]), 0)
+        collect_start(3)
+        y = collect_wait(3)
+        ybuf[1] = jnp.stack(y)
+        w = apply_inverse([inv_b[c] for c in range(6)], y)
+        wbuf[1] = jnp.stack(w)
+        spread_start(w, wsrc, recv_s, ss_sem, sr_sem)
+        spread_wait(wsrc, recv_s, ss_sem, sr_sem)
+        near = take_points(recv_s)
+        eliminate(gg[1, 0], gg[1, 1], near, 1)
+        c0 = back_to_cams(1) + cam_damp * z0
         u = c0 / precond
         first = 2 * step
-        reduce_x_start(
-            first, [lane_sum(r0 * z0), lane_sum(z0 * c0), lane_sum(c0 * u), cost_row]
-        )
-        operator(u, 2)
-        reduce_y_start(first)
-        operator_finish(u, 2)
-        q = operator_end(u, 2)
-        dots = reduce_wait(first)
+        total_start(first, [lane_sum(r0 * z0), lane_sum(z0 * c0), lane_sum(c0 * u), cost_row])
+
+        take_cams(u, 2)
+        put_points(to_points(gg[2, 0], gg[2, 1]), 0)
+        collect_start(3)
+        y = collect_wait(3)
+        ybuf[2] = jnp.stack(y)
+        w = apply_inverse([inv_b[c] for c in range(6)], y)
+        wbuf[2] = jnp.stack(w)
+
+        dots = total_wait(first)
         resid_dot, curve, square = dots[0], dots[1], dots[2]
-        cost_o[pl.ds(step, 1), :] = 0.5 * dots[3]
+        cost_o[pl.ds(step, 1), :] = jnp.broadcast_to(0.5 * dots[3], (1, LANES))
         alpha = resid_dot / curve
         beta = (resid_dot - 2.0 * alpha * curve + alpha * alpha * square) / resid_dot
-        r1 = r0 - alpha * c0
-        z1 = r1 / precond
+        more = 1.0 + beta
+        z1 = (r0 - alpha * c0) / precond
         d1 = z1 + beta * z0
-        sd1 = (1.0 + beta) * c0 - alpha * q
-        rows = [lane_sum(r1 * z1), lane_sum(d1 * sd1)]
+        turn = [more * gg[1, r] - alpha * gg[2, r] for r in range(2)]
+        y_turn = mix(more, three(ybuf, 1), -alpha, three(ybuf, 2))
+        w_turn = mix(more, three(wbuf, 1), -alpha, three(wbuf, 2))
+        turn_sq = lane_sum(turn[0] * turn[0] + turn[1] * turn[1])
+        yw = inner(y_turn, w_turn)
+        rows = [
+            lane_sum((r0 - alpha * c0) * z1),
+            turn_sq - yw + lane_sum(cam_damp * (d1 * d1)),
+        ]
         if last:
-            near = bk[0] + alpha * bk[1]
-            turn = (1.0 + beta) * bk[1] - alpha * bk[2]
-            rows += [lane_sum(near * near), lane_sum(near * turn), lane_sum(turn * turn)]
+            base = [mv[r] + alpha * gg[1, r] for r in range(2)]
+            y_base = mix(1.0, three(ybuf, 0), alpha, three(ybuf, 1))
+            w_base = mix(1.0, three(wbuf, 0), alpha, three(wbuf, 1))
+            hw_base = weighted(w_base)
+            hw_turn = weighted(w_turn)
+            rows += [
+                lane_sum(base[0] * base[0] + base[1] * base[1])
+                - 2.0 * inner(y_base, w_base)
+                + inner(w_base, hw_base),
+                lane_sum(base[0] * turn[0] + base[1] * turn[1])
+                - inner(y_base, w_turn)
+                - inner(y_turn, w_base)
+                + inner(w_base, hw_turn),
+                turn_sq - 2.0 * yw + inner(w_turn, hw_turn),
+            ]
         second = first + 1
-        reduce_x_start(second, rows)
+        total_start(second, rows)
         if not last:
             hess = [hess_b[c] for c in range(6)]
             inv = invert(hess, LAMBDAS[1])
@@ -490,17 +553,26 @@
             held = []
             for b in range(3):
                 held.append([scale[m] * wbuf[b, m] + ybuf[b, m] for m in range(3)])
-            base = [
+            y_fix = [
                 scale[m] * wbuf[0, m] + y_start[m] + alpha * held[1][m] for m in range(3)
             ]
-            move = [(1.0 + beta) * held[1][m] - alpha * held[2][m] for m in range(3)]
-            spread_start(apply_inverse(inv, base) + apply_inverse(inv, move), wsrc4, recv_s4, s4s_sem, s4r_sem)
-        reduce_y_start(second)
-        if not last:
-            spread_wait(wsrc4, recv_s4, s4s_sem, s4r_sem)
-        dots = reduce_wait(second)
+            y_move = mix(more, held[1], -alpha, held[2])
+            w_fix = apply_inverse(inv, y_fix)
+            w_move = apply_inverse(inv, y_move)
+            spread_start(w + w_fix + w_move, wsrc_w, recv_w, ws_sem, wr_sem)
+            spread_wait(wsrc_w, recv_w, ws_sem, wr_sem)
+            near = take_points(recv_w)
+            eliminate(gg[2, 0], gg[2, 1], near, 2)
+            near_fix = take_points(recv_w, 3)
+            near_move = take_points(recv_w, 6)
+        else:
+            spread_start(w, wsrc, recv_s, ss_sem, sr_sem)
+            spread_wait(wsrc, recv_s, ss_sem, sr_sem)
+            near = take_points(recv_s)
+            eliminate(gg[2, 0], gg[2, 1], near, 2)
+        dots = total_wait(second)
         alpha1 = dots[0] / dots[1]
-        ca = alpha + alpha1 * (1.0 + beta)
+        ca = alpha + alpha1 * more
         cb = -(alpha1 * alpha)
         update = update + alpha * z0 + alpha1 * d1
         upd_sum = upd_sum + update
@@ -511,21 +583,20 @@
                 rs[r] = res
                 mv[r] = res + (gg[0, r] + ca * gg[1, r] + cb * gg[2, r])
             cost_row = lane_sum(rs[...] * rs[...])
-            for n in range(9):
-                for m in range(3):
-                    comb[n, m] = recv_s4[n, m] + alpha1 * recv_s4[n, 3 + m]
-            wbuf[0] = wsrc4[0:3] + alpha1 * wsrc4[3:6]
+            near = [near_fix[m] + alpha1 * near_move[m] for m in range(3)]
+            ybuf[0] = jnp.stack(mix(1.0, y_fix, alpha1, y_move))
+            wbuf[0] = jnp.stack(mix(1.0, w_fix, alpha1, w_move))
         else:
             for r in range(2):
                 res_o[r] = bk[0, r] + ca * bk[1, r] + cb * bk[2, r]
-            cost_o[pl.ds(2, 1), :] = 0.5 * (
-                dots[2] + 2.0 * alpha1 * dots[3] + alpha1 * alpha1 * dots[4]
+            cost_o[pl.ds(2, 1), :] = jnp.broadcast_to(
+                0.5 * (dots[2] + 2.0 * alpha1 * dots[3] + alpha1 * alpha1 * dots[4]), (1, LANES)
             )
     upd_o[...] = upd_sum
     step_o[...] = step_sum
     cost_o[pl.ds(3, 5), :] = jnp.zeros((5, LANES), F32)
     for a in range(4):
-        reduce_drain(a)
+        total_drain(a)
 
 
 def body(
@@ -580,19 +651,16 @@
             pltpu.VMEM((8, 12) + blk, F32),
             pltpu.VMEM((3,) + blk, F32),
             pltpu.VMEM((9, 3) + blk, F32),
-            pltpu.VMEM((6,) + blk, F32),
-            pltpu.VMEM((9, 6) + blk, F32),
-            pltpu.VMEM((9, 3) + blk, F32),
+            pltpu.VMEM((9,) + blk, F32),
+            pltpu.VMEM((9, 9) + blk, F32),
             pltpu.VMEM((6,) + blk, F32),
             pltpu.VMEM((6,) + blk, F32),
             pltpu.VMEM((3, 3) + blk, F32),
             pltpu.VMEM((3, 3) + blk, F32),
             pltpu.VMEM((CPAR, 2, LANES), F32),
             pltpu.VMEM((CPAR, 2, LANES), F32),
-            pltpu.VMEM((4, 8, LANES), F32),
-            pltpu.VMEM((4, 8, LANES), F32),
-            pltpu.VMEM((4, GX, 8, LANES), F32),
-            pltpu.VMEM((4, GY, 8, LANES), F32),
+            pltpu.VMEM((4, 1, LANES), F32),
+            pltpu.VMEM((4, GX * GY, LANES), F32),
             dma((4,)),
             dma((8,)),
             dma((8,)),
@@ -600,10 +668,8 @@
             dma((8,)),
             dma((8,)),
             dma((8,)),
-            dma((4, GX)),
-            dma((4, GX)),
-            dma((4, GY)),
-            dma((4, GY)),
+            dma((4,)),
+            dma((4,)),
         ],
         compiler_params=pltpu.CompilerParams(
             collective_id=0, has_side_effects=True, vmem_limit_bytes=48 * 1024 * 1024

time: 127 us -> 105 us (0.83)
  Pallas kernels: 116 us -> 94 us
    pallas_call x1, Pallas kernels: 116 us -> 94 us  [body(): pl.pallas_call(kernel, out_shape=[jax.ShapeDtypeStruct((CPAR, 2, LANES),...]
where the time goes in v2:
time: 105 us
  Pallas kernels  94 us (90%)
  local copies, waits for them, and re-layouts  9.11 us (9%)
  other arithmetic  1.22 us (1%)
    pallas_call x1, Pallas kernels, body(): pl.pallas_call(kernel, out_shape=[jax.ShapeDtypeStruct((CPAR, 2, LANES),...  94 us
    unnamed x21, local copies, waits for them, and re-layouts  7.57 us

profile of v2, /device:TPU:1, one launch (start us, length us, event | category | flops | bytes accessed | tf_op | source)
XLA Modules:
  0.0 105.0 jit_solution(12797993060004401518)
XLA Ops:
  0.6 0.0 copy-start.9
  0.6 0.0 copy-start.8
  0.7 0.8 reshape.14.start_r
  1.5 0.0 copy-start
  1.5 1.3 %copy-done = f32[1,1,128,18,128]{4,2,3,1,0:T(8,128)S(1)} copy-done((f32[1,1,128,18,128]{4,2,3,1,0:T(8,128)S(1)}, f32[1,1,128,18,128]{4,2,3,1,0:T(8,128)}, u32[]{:S(2)}) %copy-start) | copy-done | bytes 1179672
  2.7 0.0 copy-start.1
  2.7 1.0 copy-done.1
  3.7 0.0 copy-start.2
  3.7 0.9 copy-done.2
  4.6 0.0 copy-start.3
  4.6 0.8 copy-done.3
  5.5 0.0 copy-start.4
  5.5 0.8 copy-done.4
  6.3 0.0 copy-start.5
  6.3 0.7 copy-done.5
  7.0 0.0 copy-start.6
  7.0 0.7 copy-done.6
  7.6 0.0 copy-start.7
  7.6 0.7 copy-done.7
  8.3 94.0 %shard_map.138 = (f32[9,2,128]{2,1,0:T(2,128)S(1)}, f32[3,16,128]{2,1,0:T(8,128)S(1)}, f32[2,128,128]{2,1,0:T(8,128)S(1)}, f32[8,128]{1,0:T(8,128)S(1)}) custom-call(s32[128]{0:T(128)S(1)} %bitcast.32, f32[18,128,128]{2,1,0:T(8,128)S(1)} %bitcast.26, f32[6,128,128]{2,1,0:T(8,128)S(1)} %bitcast.27, f32[128,2,128]{2,1,0:T(2,128)S(1)} %bitcast.29, ...), custom_call_target="tpu_custom_call" | custom-call | tf_op jit(solution)/shard_map/pallas_call | solution.py:623
  102.3 0.8 copy.16
  103.1 0.1 reshape.15
  103.2 0.0 copy-done.9
  103.2 0.6 add.6
  103.8 0.0 copy-done.8
  103.8 0.6 bitcast_add_fusion
  104.4 0.6 slice_reduce_fusion
Async XLA Ops:
  0.6 102.5 %copy-start.9 = (f32[1,1,4,9,64]{4,2,3,1,0:T(4,128)S(1)}, f32[1,1,4,9,64]{4,2,3,1,0:T(4,128)}, u32[]{:S(2)}) copy-start(f32[1,1,4,9,64]{4,2,3,1,0:T(4,128)} %param.19) | copy-start | bytes 27652
  0.6 103.1 %copy-start.8 = (f32[1,1,16,3,128]{4,2,3,1,0:T(8,128)S(1)}, f32[1,1,16,3,128]{4,2,3,1,0:T(8,128)}, u32[]{:S(2)}) copy-start(f32[1,1,16,3,128]{4,2,3,1,0:T(8,128)} %param.20) | copy-start | bytes 73732
  1.5 1.3 %copy-start = (f32[1,1,128,18,128]{4,2,3,1,0:T(8,128)S(1)}, f32[1,1,128,18,128]{4,2,3,1,0:T(8,128)}, u32[]{:S(2)}) copy-start(f32[1,1,128,18,128]{4,2,3,1,0:T(8,128)} %param.11) | copy-start | bytes 3538948
  2.7 1.0 copy-start.1
  3.7 0.9 copy-start.2
  4.6 0.8 copy-start.3
  5.5 0.8 copy-start.4
  6.3 0.7 copy-start.5
  7.0 0.7 copy-start.6
  7.6 0.7 copy-start.7

commit v3 on v2

--- a/solution.py
+++ b/solution.py
@@ -13,6 +13,7 @@
 SLOTS = 9 * NBLK
 GX = 8
 GY = 16
+PAD = 64
 STEPS = (1, 2, 4, 8, 16, 32, 64)
 LAMBDAS = (1.0, 0.25)
 PAIRS = ((0, 0), (0, 1), (0, 2), (1, 1), (1, 2), (2, 2))
@@ -99,12 +100,12 @@
     jc_h,
     jp_h,
     rs_h,
-    obs_cam,
-    obs_pt,
-    count_r,
-    tcam_r,
-    tpts_r,
-    start_r,
+    cam_h,
+    pt_h,
+    count_h,
+    tcam_h,
+    tpts_h,
+    start_h,
     upd_o,
     step_o,
     res_o,
@@ -112,6 +113,17 @@
     jc,
     jp,
     rs,
+    obs_cam,
+    obs_pt,
+    count_r,
+    tcam_r,
+    tpts_r,
+    start_r,
+    jct,
+    jpt,
+    seg_t,
+    scan_a,
+    scan_b,
     perm,
     endi,
     smask,
@@ -120,17 +132,20 @@
     pair_m,
     idx_c,
     onehot,
-    zbuf,
     table,
     gg,
     bk,
     mv,
     contrib,
     recv_c,
+    contrib_y,
+    recv_y,
     wsrc,
     recv_s,
     wsrc_w,
     recv_w,
+    wsrc_2,
+    recv_2,
     hess_b,
     inv_b,
     ybuf,
@@ -142,10 +157,14 @@
     in_sem,
     cs_sem,
     cr_sem,
+    ys_sem,
+    yr_sem,
     ss_sem,
     sr_sem,
     ws_sem,
     wr_sem,
+    s2_sem,
+    r2_sem,
     as_sem,
     ar_sem,
 ):
@@ -173,6 +192,24 @@
         for dx in (4, 3, 5, 2, 6, 1, 7):
             act(dx, 0)
 
+    pairs = [
+        (pt_h, obs_pt),
+        (jp_h, jp),
+        (jc_h, jc),
+        (cam_h, obs_cam),
+        (rs_h.at[:, 0, :], rs.at[0]),
+        (rs_h.at[:, 1, :], rs.at[1]),
+        (tcam_h, tcam_r),
+        (count_h, count_r),
+        (tpts_h, tpts_r),
+        (start_h, start_r),
+    ]
+    copies = [
+        pltpu.make_async_copy(src, dst, in_sem.at[i]) for i, (src, dst) in enumerate(pairs)
+    ]
+    for copy in copies:
+        copy.start()
+
     for r, n in enumerate(OTHERS):
 
         @pl.when(jnp.logical_not(here[n]))
@@ -180,6 +217,8 @@
             recv_c[r] = jnp.zeros_like(recv_c[r])
             recv_s[n] = jnp.zeros_like(recv_s[n])
             recv_w[n] = jnp.zeros_like(recv_w[n])
+            recv_2[n] = jnp.zeros_like(recv_2[n])
+            recv_y[r] = jnp.zeros_like(recv_y[r])
 
     barrier = pltpu.get_barrier_semaphore()
     to_all(
@@ -188,56 +227,48 @@
         )
     )
 
-    copies = [
-        pltpu.make_async_copy(rs_h.at[:, 0, :], rs.at[0], in_sem.at[0]),
-        pltpu.make_async_copy(rs_h.at[:, 1, :], rs.at[1], in_sem.at[1]),
-        pltpu.make_async_copy(jp_h, jp, in_sem.at[2]),
-        pltpu.make_async_copy(jc_h, jc, in_sem.at[3]),
-    ]
-    for copy in copies:
-        copy.start()
-
+    seg_t[0:PAD, :] = jnp.full((PAD, LANES), -1.0, F32)
+    for k in range(CPAR):
+        scan_a[k, 0:PAD, :] = jnp.zeros((PAD, LANES), F32)
+        scan_b[k, 0:PAD, :] = jnp.zeros((PAD, LANES), F32)
     lane = lane_ids(TILES)
-    tcam = column(tcam_r[...]).astype(jnp.int32)
-    parity = tcam & 1
-    pair = tcam >> 1
-    pair_m[...] = pair
-    idx_c[...] = parity * 64 + obs_cam[...]
-
-    def order(kind):
-        ids = obs_pt[...] if kind == 0 else obs_cam[...]
+
+    def order(kind, ids, target):
         key = sort_lanes(ids * LANES + lane)
         perm[kind] = key & (LANES - 1)
         seg = key >> 7
-        for i, d in enumerate(STEPS):
-            same = (pltpu.roll(seg, d, axis=1) == seg) & (lane >= d)
-            smask[kind, i] = jnp.where(same, 1.0, 0.0)
-        target = lane if kind == 0 else lane & 63
         count = last_at_most(seg, target)
         last = jnp.maximum(count - 1, 0)
         endi[kind] = last
         found = (count > 0) & (pick(seg, last) == target)
-        if kind == 0:
-            hit_p[...] = jnp.where(found, 1.0, 0.0)
-        else:
-            mine = found & ((lane >> 6) == parity)
-            hit_c[0] = jnp.where(mine & (pair == 0), 1.0, 0.0)
-            hit_c[1] = jnp.where(mine & (pair == 1), 1.0, 0.0)
-
-    order(0)
-    slot_row = lax.broadcasted_iota(jnp.int32, (SLOTS, TILES), 0)
-    hot = jnp.where(slot_row == tpts_r[...], 1.0, 0.0).astype(BF16)
-    for i in range(3):
-        onehot[:, i * TILES : (i + 1) * TILES] = hot
-
-    def summed(x, kind):
-        x = pick(x, perm[kind])
+        seg_t[PAD : PAD + LANES, :] = jnp.swapaxes(seg.astype(F32), 0, 1)
         for i, d in enumerate(STEPS):
-            x = x + pltpu.roll(x, d, axis=1) * smask[kind, i]
-        return pick(x, endi[kind])
-
-    def put_points(values, first):
-        sums = jnp.concatenate([summed(v, 0) * hit_p[...] for v in values], axis=1)
+            same = seg_t[PAD : PAD + LANES, :] == seg_t[PAD - d : PAD + LANES - d, :]
+            smask[kind, i] = jnp.where(same, 1.0, 0.0)
+        return found
+
+    def sorted_t(x, kind):
+        return jnp.swapaxes(pick(x, perm[kind]), 0, 1)
+
+    def summed(values, kind):
+        count = len(values)
+        src, dst = scan_a, scan_b
+        for k in range(count):
+            src[k, PAD : PAD + LANES, :] = values[k]
+        for i, d in enumerate(STEPS):
+            for k in range(count):
+                dst[k, PAD : PAD + LANES, :] = (
+                    src[k, PAD : PAD + LANES, :]
+                    + src[k, PAD - d : PAD + LANES - d, :] * smask[kind, i]
+                )
+            src, dst = dst, src
+        return [
+            pick(jnp.swapaxes(src[k, PAD : PAD + LANES, :], 0, 1), endi[kind])
+            for k in range(count)
+        ]
+
+    def put_points(values, first, dest):
+        sums = jnp.concatenate([v * hit_p[...] for v in summed(values, 0)], axis=1)
         high = sums.astype(BF16)
         rest = sums - high.astype(F32)
         mid = rest.astype(BF16)
@@ -246,21 +277,15 @@
         out = jnp.dot(onehot[...], parts, preferred_element_type=F32)
         for n in range(9):
             for m in range(3):
-                contrib[n, first + m] = out[
+                dest[n, first + m] = out[
                     n * NBLK : (n + 1) * NBLK, m * LANES : (m + 1) * LANES
                 ]
 
-    def put_cams(value_at):
-        def one(group, carry):
-            for j in range(3):
-                k = group * 3 + j
-                sums = summed(value_at(k), 1)
-                top = lane_sum(sums * hit_c[0])
-                bottom = lane_sum(sums * hit_c[1])
-                camacc[k] = jnp.concatenate([top, bottom], axis=0)
-            return carry
-
-        lax.fori_loop(0, 3, one, 0)
+    def put_cams(values):
+        for k, sums in enumerate(summed(values, 1)):
+            top = lane_sum(sums * hit_c[0])
+            bottom = lane_sum(sums * hit_c[1])
+            camacc[k] = jnp.concatenate([top, bottom], axis=0)
         return camacc[...]
 
     def take_cams(vector, b):
@@ -290,40 +315,47 @@
         lax.fori_loop(0, TILES // rows, one, 0)
 
     def to_points(e0, e1):
-        return [jp[m] * e0 + jp[3 + m] * e1 for m in range(3)]
-
-    def collect_start(comps):
+        t0, t1 = sorted_t(e0, 0), sorted_t(e1, 0)
+        return [jpt[m] * t0 + jpt[3 + m] * t1 for m in range(3)]
+
+    def collect_start(comps, src, dst, send_sem, recv_sem):
         for r, n in ORDER:
             a, b = divmod(n, 3)
 
             @pl.when(here[n])
             def _(r=r, n=n, a=a, b=b):
                 pltpu.make_async_remote_copy(
-                    src_ref=contrib.at[n, pl.ds(0, comps)],
-                    dst_ref=recv_c.at[r, pl.ds(0, comps)],
-                    send_sem=cs_sem.at[r],
-                    recv_sem=cr_sem.at[r],
+                    src_ref=src.at[n, pl.ds(0, comps)],
+                    dst_ref=dst.at[r, pl.ds(0, comps)],
+                    send_sem=send_sem.at[r],
+                    recv_sem=recv_sem.at[r],
                     device_id=at(a - 1, b - 1),
                     device_id_type=MESH,
                 ).start()
 
-    def collect_wait(comps):
-        for sem, flip in ((cr_sem, True), (cs_sem, False)):
+    def collect_wait(comps, src, dst, send_sem, recv_sem):
+        for sem, flip in ((recv_sem, True), (send_sem, False)):
             for r, n in enumerate(OTHERS):
 
                 @pl.when(here[8 - n] if flip else here[n])
                 def _(r=r, n=n, sem=sem):
                     pltpu.make_async_copy(
-                        contrib.at[n, pl.ds(0, comps)], recv_c.at[r, pl.ds(0, comps)], sem.at[r]
+                        src.at[n, pl.ds(0, comps)], dst.at[r, pl.ds(0, comps)], sem.at[r]
                     ).wait()
 
         total = []
         for m in range(comps):
-            s = contrib[4, m]
+            s = src[4, m]
             for r in range(8):
-                s = s + recv_c[r, m]
+                s = s + dst[r, m]
             total.append(s)
         return total
+
+    pts = (contrib, recv_c, cs_sem, cr_sem)
+    pts_y = (contrib_y, recv_y, ys_sem, yr_sem)
+    out_s = (wsrc, recv_s, ss_sem, sr_sem)
+    out_w = (wsrc_w, recv_w, ws_sem, wr_sem)
+    out_2 = (wsrc_2, recv_2, s2_sem, r2_sem)
 
     def spread_start(values, src, dst, send_sem, recv_sem):
         for m, v in enumerate(values):
@@ -370,7 +402,8 @@
         bk[b, 1] = e1 - (jp[3] * near[0] + jp[4] * near[1] + jp[5] * near[2])
 
     def back_to_cams(b):
-        return put_cams(lambda k: jc[k] * bk[b, 0] + jc[CPAR + k] * bk[b, 1])
+        t0, t1 = sorted_t(bk[b, 0], 1), sorted_t(bk[b, 1], 1)
+        return put_cams([jct[k] * t0 + jct[CPAR + k] * t1 for k in range(CPAR)])
 
     def total_start(a, rows):
         held = jnp.concatenate(rows + [jnp.zeros((8 - len(rows), LANES), F32)], axis=0)
@@ -408,47 +441,63 @@
             arx.at[a, pl.ds(0, 127)], arx.at[a, pl.ds(0, 127)], as_sem.at[a]
         ).wait()
 
+    copies[0].wait()
+    hit_p[...] = jnp.where(order(0, obs_pt[...], lane), 1.0, 0.0)
+    for copy in copies[1:]:
+        copy.wait()
+    slot_row = lax.broadcasted_iota(jnp.int32, (SLOTS, TILES), 0)
+    hot = jnp.where(slot_row == tpts_r[...], 1.0, 0.0).astype(BF16)
+    for i in range(3):
+        onehot[:, i * TILES : (i + 1) * TILES] = hot
+    tcam = column(tcam_r[...]).astype(jnp.int32)
+    parity = tcam & 1
+    pair = tcam >> 1
+    pair_m[...] = pair
+    idx_c[...] = parity * 64 + obs_cam[...]
+
     valid = jnp.where(lane < column(count_r[...]).astype(jnp.int32), 1.0, 0.0)
-    for copy in copies:
-        copy.wait()
     for k in range(2):
         rs[k] = rs[k] * valid
     for k in range(6):
         jp[k] = jp[k] * valid
+        jpt[k] = sorted_t(jp[k], 0)
     for k in range(18):
         jc[k] = jc[k] * valid
-
-    start = start_r[...]
+    square = [jpt[i] * jpt[j] + jpt[3 + i] * jpt[3 + j] for i, j in PAIRS]
+    put_points(square[0:3], 0, contrib)
+    put_points(square[3:6], 3, contrib)
+
+    start = jnp.concatenate(
+        [
+            jnp.concatenate([start_r[:, 2 * p, :], start_r[:, 2 * p + 1, :]], axis=1)[:, None, :]
+            for p in range(2)
+        ],
+        axis=1,
+    )
     take_cams(start, 0)
-
-    for c, (i, j) in enumerate(PAIRS):
-        zbuf[c] = jp[i] * jp[j] + jp[3 + i] * jp[3 + j]
-    for m, v in enumerate(to_points(rs[0], rs[1])):
-        zbuf[6 + m] = v
-    for m, v in enumerate(to_points(gg[0, 0], gg[0, 1])):
-        zbuf[9 + m] = v
-
-    def first_points(group, carry):
-        put_points([zbuf[group * 3 + m] for m in range(3)], group * 3)
-        return carry
-
-    lax.fori_loop(0, 4, first_points, 0)
+    for k in range(2):
+        mv[k] = rs[k] + gg[0, k]
+    put_points(to_points(mv[0], mv[1]), 6, contrib)
     pl.semaphore_wait(barrier, GX * GY - 1)
-    collect_start(12)
-    order(1)
-    diag = put_cams(lambda k: jc[k] * jc[k] + jc[CPAR + k] * jc[CPAR + k])
+    collect_start(9, *pts)
+    put_points(to_points(gg[0, 0], gg[0, 1]), 0, contrib_y)
+    collect_start(3, *pts_y)
+    found = order(1, obs_cam[...], lane & 63)
+    mine = found & ((lane >> 6) == parity)
+    hit_c[0] = jnp.where(mine & (pair == 0), 1.0, 0.0)
+    hit_c[1] = jnp.where(mine & (pair == 1), 1.0, 0.0)
+    for k in range(18):
+        jct[k] = sorted_t(jc[k], 1)
+    diag = put_cams([jct[k] * jct[k] + jct[CPAR + k] * jct[CPAR + k] for k in range(CPAR)])
     cost_row = lane_sum(rs[...] * rs[...])
-    owned = collect_wait(12)
+    owned = collect_wait(9, *pts)
     for c in range(6):
         hess_b[c] = owned[c]
-    y_start = owned[9:12]
-    ybuf[0] = jnp.stack([owned[6 + m] + owned[9 + m] for m in range(3)])
+    ybuf[0] = jnp.stack(owned[6:9])
 
     update = start
     upd_sum = jnp.zeros_like(start)
     step_sum = jnp.zeros((3, NBLK, LANES), F32)
-    for k in range(2):
-        mv[k] = rs[k] + gg[0, k]
 
     def weighted(w):
         h = [hess_b[c] for c in range(6)]
@@ -472,8 +521,8 @@
         inv_b[c] = inv[c]
     w0 = apply_inverse(inv, three(ybuf, 0))
     wbuf[0] = jnp.stack(w0)
-    spread_start(w0, wsrc, recv_s, ss_sem, sr_sem)
-    spread_wait(wsrc, recv_s, ss_sem, sr_sem)
+    spread_start(w0, *out_s)
+    spread_wait(*out_s)
     near = take_points(recv_s)
 
     for step in range(2):
@@ -481,19 +530,29 @@
         last = step == 1
         cam_damp = damping * (diag + 1.0)
         precond = diag + cam_damp
-        eliminate(mv[0], mv[1], near, 0)
+        if step == 0:
+            eliminate(mv[0], mv[1], near, 0)
         r0 = -back_to_cams(0) - cam_damp * update
         z0 = r0 / precond
 
         take_cams(z0, 1)
-        put_points(to_points(gg[1, 0], gg[1, 1]), 0)
-        collect_start(3)
-        y = collect_wait(3)
+        put_points(to_points(gg[1, 0], gg[1, 1]), 0, contrib)
+        collect_start(3, *pts)
+        if last:
+            spread_wait(*out_2)
+            near = take_points(recv_2)
+            for r in range(2):
+                shift = jp[3 * r] * near[0] + jp[3 * r + 1] * near[1] + jp[3 * r + 2] * near[2]
+                res = rs[r] - cb * shift
+                rs[r] = res
+                mv[r] = mv[r] + res
+            cost_row = lane_sum(rs[...] * rs[...])
+        y = collect_wait(3, *pts)
         ybuf[1] = jnp.stack(y)
         w = apply_inverse([inv_b[c] for c in range(6)], y)
         wbuf[1] = jnp.stack(w)
-        spread_start(w, wsrc, recv_s, ss_sem, sr_sem)
-        spread_wait(wsrc, recv_s, ss_sem, sr_sem)
+        spread_start(w, *out_s)
+        spread_wait(*out_s)
         near = take_points(recv_s)
         eliminate(gg[1, 0], gg[1, 1], near, 1)
         c0 = back_to_cams(1) + cam_damp * z0
@@ -502,9 +561,9 @@
         total_start(first, [lane_sum(r0 * z0), lane_sum(z0 * c0), lane_sum(c0 * u), cost_row])
 
         take_cams(u, 2)
-        put_points(to_points(gg[2, 0], gg[2, 1]), 0)
-        collect_start(3)
-        y = collect_wait(3)
+        put_points(to_points(gg[2, 0], gg[2, 1]), 0, contrib)
+        collect_start(3, *pts)
+        y = collect_wait(3, *pts)
         ybuf[2] = jnp.stack(y)
         w = apply_inverse([inv_b[c] for c in range(6)], y)
         wbuf[2] = jnp.stack(w)
@@ -553,21 +612,21 @@
             held = []
             for b in range(3):
                 held.append([scale[m] * wbuf[b, m] + ybuf[b, m] for m in range(3)])
+            y_start = collect_wait(3, *pts_y)
             y_fix = [
                 scale[m] * wbuf[0, m] + y_start[m] + alpha * held[1][m] for m in range(3)
             ]
             y_move = mix(more, held[1], -alpha, held[2])
             w_fix = apply_inverse(inv, y_fix)
             w_move = apply_inverse(inv, y_move)
-            spread_start(w + w_fix + w_move, wsrc_w, recv_w, ws_sem, wr_sem)
-            spread_wait(wsrc_w, recv_w, ws_sem, wr_sem)
-            near = take_points(recv_w)
-            eliminate(gg[2, 0], gg[2, 1], near, 2)
-            near_fix = take_points(recv_w, 3)
-            near_move = take_points(recv_w, 6)
+            spread_start(w_fix + mix(1.0, w_move, -alpha, w), *out_w)
+            spread_start(w, *out_2)
+            spread_wait(*out_w)
+            near_fix = take_points(recv_w)
+            near_move = take_points(recv_w, 3)
         else:
-            spread_start(w, wsrc, recv_s, ss_sem, sr_sem)
-            spread_wait(wsrc, recv_s, ss_sem, sr_sem)
+            spread_start(w, *out_s)
+            spread_wait(*out_s)
             near = take_points(recv_s)
             eliminate(gg[2, 0], gg[2, 1], near, 2)
         dots = total_wait(second)
@@ -578,12 +637,11 @@
         upd_sum = upd_sum + update
         step_sum = step_sum - (wbuf[0] + ca * wbuf[1] + cb * wbuf[2])
         if not last:
+            near = [near_fix[m] + alpha1 * near_move[m] for m in range(3)]
             for r in range(2):
-                res = bk[0, r] + ca * bk[1, r] + cb * bk[2, r]
-                rs[r] = res
-                mv[r] = res + (gg[0, r] + ca * gg[1, r] + cb * gg[2, r])
-            cost_row = lane_sum(rs[...] * rs[...])
-            near = [near_fix[m] + alpha1 * near_move[m] for m in range(3)]
+                rs[r] = bk[0, r] + ca * bk[1, r] + cb * gg[2, r]
+                mv[r] = gg[0, r] + ca * gg[1, r] + cb * gg[2, r]
+            eliminate(rs[0] + mv[0], rs[1] + mv[1], near, 0)
             ybuf[0] = jnp.stack(mix(1.0, y_fix, alpha1, y_move))
             wbuf[0] = jnp.stack(mix(1.0, w_fix, alpha1, w_move))
         else:
@@ -612,9 +670,6 @@
     pt_params,
     cg_start,
 ):
-    start = jnp.transpose(
-        cg_start[0, 0].reshape(2, 2, CPAR, 64), (2, 0, 1, 3)
-    ).reshape(CPAR, 2, LANES)
     vmem = pl.BlockSpec(memory_space=pltpu.VMEM)
     hbm = pl.BlockSpec(memory_space=pl.ANY)
     big = (TILES, LANES)
@@ -628,12 +683,23 @@
             jax.ShapeDtypeStruct((2,) + big, F32),
             jax.ShapeDtypeStruct((8, LANES), F32),
         ],
-        in_specs=[pl.BlockSpec(memory_space=pltpu.SMEM)] + [hbm] * 3 + [vmem] * 6,
+        in_specs=[pl.BlockSpec(memory_space=pltpu.SMEM)] + [hbm] * 9,
         out_specs=[vmem] * 4,
         scratch_shapes=[
             pltpu.VMEM((18,) + big, F32),
             pltpu.VMEM((6,) + big, F32),
             pltpu.VMEM((2,) + big, F32),
+            pltpu.VMEM(big, jnp.int32),
+            pltpu.VMEM(big, jnp.int32),
+            pltpu.VMEM((1, LANES), jnp.int32),
+            pltpu.VMEM((1, LANES), jnp.int32),
+            pltpu.VMEM((1, LANES), jnp.int32),
+            pltpu.VMEM((CPAR, 4, 64), F32),
+            pltpu.VMEM((18,) + big, F32),
+            pltpu.VMEM((6,) + big, F32),
+            pltpu.VMEM((PAD + LANES, LANES), F32),
+            pltpu.VMEM((CPAR, PAD + LANES, LANES), F32),
+            pltpu.VMEM((CPAR, PAD + LANES, LANES), F32),
             pltpu.VMEM((2,) + big, jnp.int32),
             pltpu.VMEM((2,) + big, jnp.int32),
             pltpu.VMEM((2, 7) + big, F32),
@@ -642,17 +708,20 @@
             pltpu.VMEM(big, jnp.int32),
             pltpu.VMEM(big, jnp.int32),
             pltpu.VMEM((SLOTS, 3 * TILES), BF16),
-            pltpu.VMEM((12,) + big, F32),
             pltpu.VMEM((3,) + big, F32),
             pltpu.VMEM((3, 2) + big, F32),
             pltpu.VMEM((3, 2) + big, F32),
             pltpu.VMEM((2,) + big, F32),
-            pltpu.VMEM((9, 12) + blk, F32),
-            pltpu.VMEM((8, 12) + blk, F32),
+            pltpu.VMEM((9, 9) + blk, F32),
+            pltpu.VMEM((8, 9) + blk, F32),
+            pltpu.VMEM((9, 3) + blk, F32),
+            pltpu.VMEM((8, 3) + blk, F32),
             pltpu.VMEM((3,) + blk, F32),
             pltpu.VMEM((9, 3) + blk, F32),
-            pltpu.VMEM((9,) + blk, F32),
-            pltpu.VMEM((9, 9) + blk, F32),
+            pltpu.VMEM((6,) + blk, F32),
+            pltpu.VMEM((9, 6) + blk, F32),
+            pltpu.VMEM((3,) + blk, F32),
+            pltpu.VMEM((9, 3) + blk, F32),
             pltpu.VMEM((6,) + blk, F32),
             pltpu.VMEM((6,) + blk, F32),
             pltpu.VMEM((3, 3) + blk, F32),
@@ -661,18 +730,12 @@
             pltpu.VMEM((CPAR, 2, LANES), F32),
             pltpu.VMEM((4, 1, LANES), F32),
             pltpu.VMEM((4, GX * GY, LANES), F32),
-            dma((4,)),
-            dma((8,)),
-            dma((8,)),
-            dma((8,)),
-            dma((8,)),
-            dma((8,)),
-            dma((8,)),
-            dma((4,)),
-            dma((4,)),
-        ],
+            dma((10,)),
+        ]
+        + [dma((8,))] * 10
+        + [dma((4,))] * 2,
         compiler_params=pltpu.CompilerParams(
-            collective_id=0, has_side_effects=True, vmem_limit_bytes=48 * 1024 * 1024
+            collective_id=0, has_side_effects=True, vmem_limit_bytes=62 * 1024 * 1024
         ),
     )(
         tile_points[0, 0],
@@ -684,7 +747,7 @@
         obs_count[0],
         tile_camera[0],
         tile_points[0],
-        start,
+        jnp.transpose(cg_start[0, 0], (1, 0, 2)),
     )
     moved = jnp.transpose(upd.reshape(CPAR, 2, 2, 64), (1, 2, 0, 3)).reshape(4, CPAR, 64)
     cam_out = cam_params + moved[None, None]

time: 105 us -> 91 us (0.87)
  Pallas kernels: 94 us -> 84.3 us
  local copies, waits for them, and re-layouts: 9.11 us -> 3.76 us
    pallas_call x1, Pallas kernels: 94 us -> 84.3 us  [body(): pl.pallas_call(kernel, out_shape=[jax.ShapeDtypeStruct((CPAR, 2, LANES),...]
    unnamed x21 -> x5, local copies, waits for them, and re-layouts: 7.57 us -> 1.67 us
where the time goes in v3:
time: 91 us; the launch traced here: 90.7 us
  Pallas kernels  84.3 us (93%)
  local copies, waits for them, and re-layouts  3.76 us (4%)
  other arithmetic  1.96 us (2%)
    pallas_call x1, Pallas kernels, body(): pl.pallas_call(kernel, out_shape=[jax.ShapeDtypeStruct((CPAR, 2, LANES),...  84.3 us

profile of v3, /device:TPU:1, one launch (start us, length us, event | category | flops | bytes accessed | tf_op | source)
XLA Modules:
  0.0 90.7 jit_solution(18198574890253531498)
XLA Ops:
  0.6 0.0 copy-start.1
  0.6 0.0 copy-start
  0.7 84.3 %shard_map.138 = (f32[9,2,128]{2,1,0:T(2,128)}, f32[3,16,128]{2,1,0:T(8,128)}, f32[2,128,128]{2,1,0:T(8,128)}, f32[8,128]{1,0:T(8,128)}) custom-call(s32[128]{0:T(128)} %bitcast.34, f32[18,128,128]{2,1,0:T(8,128)} %bitcast.26, f32[6,128,128]{2,1,0:T(8,128)} %bitcast.27, f32[128,2,128]{2,1,0:T(2,128)} %bitcast.28, s32[128,128]{1,0:T(8,128)} %bitcast.31, ...), custom_call_target="tpu_custom_call" | custom-call | tf_op jit(solution)/shard_map/pallas_call | solution.py:678
  85.0 1.7 %copy.16 = f32[1,1,128,2,128]{4,3,2,1,0:T(2,128)} copy(f32[1,1,128,2,128]{4,2,3,1,0:T(8,128)} %bitcast.29) | data formatting | bytes 262144
  86.6 0.8 reshape.11
  87.4 0.0 copy-done.1
  87.4 0.6 add.6
  88.0 0.0 copy-done
  88.0 1.3 %bitcast_add_fusion = f32[1,1,16,3,128]{4,2,3,1,0:T(8,128)} fusion(f32[1,1,16,3,128]{4,2,3,1,0:T(8,128)S(1)} %copy-done, f32[3,16,128]{2,1,0:T(8,128)} %get-tuple-element.9), kind=kLoop, calls=%fused_computation | loop fusion | flops 6144 | bytes 73728 | tf_op jit(solution)/shard_map/add | solution.py:754
  89.4 1.3 %slice_reduce_fusion = f32[3]{0:T(128)} fusion(f32[8,128]{1,0:T(8,128)} %get-tuple-element.11), kind=kLoop, calls=%fused_computation.1 | loop fusion | bytes 24 | tf_op jit(solution)/shard_map/slice | solution.py:756
Async XLA Ops:
  0.6 86.8 %copy-start.1 = (f32[1,1,4,9,64]{4,2,3,1,0:T(4,128)S(1)}, f32[1,1,4,9,64]{4,2,3,1,0:T(4,128)}, u32[]{:S(2)}) copy-start(f32[1,1,4,9,64]{4,2,3,1,0:T(4,128)} %param.19) | copy-start | bytes 27652
  0.6 87.4 %copy-start = (f32[1,1,16,3,128]{4,2,3,1,0:T(8,128)S(1)}, f32[1,1,16,3,128]{4,2,3,1,0:T(8,128)}, u32[]{:S(2)}) copy-start(f32[1,1,16,3,128]{4,2,3,1,0:T(8,128)} %param.20) | copy-start | bytes 73732

commit v4 on v3

--- a/solution.py
+++ b/solution.py
@@ -41,17 +41,41 @@
 
 
 def sort_lanes(key):
-    lane = lane_ids(key.shape[0])
+    flat = jnp.swapaxes(key.astype(F32), 0, 1).reshape(16, 8, LANES)
+    regs = [flat[v] for v in range(16)]
+    sub = lax.broadcasted_iota(jnp.int32, (8, LANES), 0)
+    before = None
     size = 2
     while size <= LANES:
+        if size >= 16:
+            bit = size // 16
+            sign = jnp.where((sub & bit) == 0, 1.0, -1.0)
+            turn = sign if before is None else sign * before
+            regs = [x * turn for x in regs]
+            before = sign
         gap = size // 2
         while gap >= 1:
-            other = pick(key, lane ^ gap)
-            keep_low = ((lane & gap) == 0) == ((lane & size) == 0)
-            key = jnp.where(keep_low, jnp.minimum(key, other), jnp.maximum(key, other))
+            if gap < 16:
+                for v in range(16):
+                    if v & gap == 0:
+                        low = jnp.minimum(regs[v], regs[v + gap])
+                        high = jnp.maximum(regs[v], regs[v + gap])
+                        up = size >= 16 or v & size == 0
+                        regs[v], regs[v + gap] = (low, high) if up else (high, low)
+            else:
+                g = gap // 16
+                first = (sub & g) == 0
+                for v in range(16):
+                    x = regs[v]
+                    other = jnp.where(
+                        first, pltpu.roll(x, 8 - g, axis=0), pltpu.roll(x, g, axis=0)
+                    )
+                    regs[v] = jnp.where(first, jnp.minimum(x, other), jnp.maximum(x, other))
             gap //= 2
         size *= 2
-    return key
+    rows = jnp.swapaxes(jnp.concatenate(regs, axis=0), 0, 1)
+    lane = lane_ids(LANES)
+    return pick(rows, (lane & 15) * 8 + (lane >> 4)).astype(jnp.int32)
 
 
 def last_at_most(seg, target):
@@ -106,19 +130,24 @@
     tcam_h,
     tpts_h,
     start_h,
-    upd_o,
-    step_o,
+    cpar_h,
+    ppar_h,
+    cam_o,
+    pt_o,
     res_o,
     cost_o,
     jc,
     jp,
     rs,
+    rs_in,
     obs_cam,
     obs_pt,
     count_r,
     tcam_r,
     tpts_r,
     start_r,
+    cam_r,
+    pt_r,
     jct,
     jpt,
     seg_t,
@@ -154,6 +183,10 @@
     camacc,
     ar_src,
     arx,
+    px_src,
+    px_dst,
+    py_src,
+    py_dst,
     in_sem,
     cs_sem,
     cr_sem,
@@ -167,6 +200,10 @@
     r2_sem,
     as_sem,
     ar_sem,
+    pxs_sem,
+    pxr_sem,
+    pys_sem,
+    pyr_sem,
 ):
     me_x = lax.axis_index("gx")
     me_y = lax.axis_index("gy")
@@ -197,12 +234,13 @@
         (jp_h, jp),
         (jc_h, jc),
         (cam_h, obs_cam),
-        (rs_h.at[:, 0, :], rs.at[0]),
-        (rs_h.at[:, 1, :], rs.at[1]),
+        (rs_h, rs_in),
         (tcam_h, tcam_r),
         (count_h, count_r),
         (tpts_h, tpts_r),
         (start_h, start_r),
+        (cpar_h, cam_r),
+        (ppar_h, pt_r),
     ]
     copies = [
         pltpu.make_async_copy(src, dst, in_sem.at[i]) for i, (src, dst) in enumerate(pairs)
@@ -405,12 +443,58 @@
         t0, t1 = sorted_t(bk[b, 0], 1), sorted_t(bk[b, 1], 1)
         return put_cams([jct[k] * t0 + jct[CPAR + k] * t1 for k in range(CPAR)])
 
-    def total_start(a, rows):
+    def lane_row(rows):
         held = jnp.concatenate(rows + [jnp.zeros((8 - len(rows), LANES), F32)], axis=0)
         sums = jnp.sum(held, axis=1, keepdims=True)
-        lane8 = lane_ids(8)
         own = lax.broadcasted_iota(jnp.int32, (8, LANES), 0)
-        row = jnp.sum(jnp.where(lane8 == own, sums, 0.0), axis=0, keepdims=True)
+        return jnp.sum(jnp.where(lane_ids(8) == own, sums, 0.0), axis=0, keepdims=True)
+
+    def apart(row):
+        lane1 = lane_ids(1)
+        return [
+            jnp.sum(jnp.where(lane1 == i, row, 0.0), axis=1, keepdims=True) for i in range(8)
+        ]
+
+    def pass_start(src, dst, spot, peers, send_sem, recv_sem):
+        for dx, dy in peers:
+            pltpu.make_async_remote_copy(
+                src_ref=src,
+                dst_ref=dst.at[pl.ds(spot, 1)],
+                send_sem=send_sem,
+                recv_sem=recv_sem,
+                device_id=at(dx, dy),
+                device_id_type=MESH,
+            ).start()
+
+    def hidden_start(a, rows):
+        row = lane_row(rows)
+        px_src[a] = row
+        px_dst[a, pl.ds(me_x, 1), :] = row
+        peers = [(d, 0) for d in (4, 3, 5, 2, 6, 1, 7)]
+        pass_start(px_src.at[a], px_dst.at[a], me_x, peers, pxs_sem.at[a], pxr_sem.at[a])
+
+    def hidden_turn(a):
+        rest = px_dst.at[a, pl.ds(0, GX - 1)]
+        pltpu.make_async_copy(rest, rest, pxr_sem.at[a]).wait()
+        row = jnp.sum(px_dst[a], axis=0, keepdims=True)
+        py_src[a] = row
+        py_dst[a, pl.ds(me_y, 1), :] = row
+        peers = [(0, d) for d in (8, 7, 9, 6, 10, 5, 11, 4, 12, 3, 13, 2, 14, 1, 15)]
+        pass_start(py_src.at[a], py_dst.at[a], me_y, peers, pys_sem.at[a], pyr_sem.at[a])
+
+    def hidden_wait(a):
+        rest = py_dst.at[a, pl.ds(0, GY - 1)]
+        pltpu.make_async_copy(rest, rest, pyr_sem.at[a]).wait()
+        return apart(jnp.sum(py_dst[a], axis=0, keepdims=True))
+
+    def hidden_drain(a):
+        rest = px_dst.at[a, pl.ds(0, GX - 1)]
+        pltpu.make_async_copy(rest, rest, pxs_sem.at[a]).wait()
+        rest = py_dst.at[a, pl.ds(0, GY - 1)]
+        pltpu.make_async_copy(rest, rest, pys_sem.at[a]).wait()
+
+    def total_start(a, rows):
+        row = lane_row(rows)
         ar_src[a] = row
         arx[a, pl.ds(me, 1), :] = row
 
@@ -430,11 +514,7 @@
         pltpu.make_async_copy(
             arx.at[a, pl.ds(0, 127)], arx.at[a, pl.ds(0, 127)], ar_sem.at[a]
         ).wait()
-        row = jnp.sum(arx[a], axis=0, keepdims=True)
-        lane1 = lane_ids(1)
-        return [
-            jnp.sum(jnp.where(lane1 == i, row, 0.0), axis=1, keepdims=True) for i in range(8)
-        ]
+        return apart(jnp.sum(arx[a], axis=0, keepdims=True))
 
     def total_drain(a):
         pltpu.make_async_copy(
@@ -457,7 +537,7 @@
 
     valid = jnp.where(lane < column(count_r[...]).astype(jnp.int32), 1.0, 0.0)
     for k in range(2):
-        rs[k] = rs[k] * valid
+        rs[k] = rs_in[pl.ds(k, TILES, stride=2), :] * valid
     for k in range(6):
         jp[k] = jp[k] * valid
         jpt[k] = sorted_t(jp[k], 0)
@@ -495,6 +575,7 @@
         hess_b[c] = owned[c]
     ybuf[0] = jnp.stack(owned[6:9])
 
+    costs = []
     update = start
     upd_sum = jnp.zeros_like(start)
     step_sum = jnp.zeros((3, NBLK, LANES), F32)
@@ -557,20 +638,21 @@
         eliminate(gg[1, 0], gg[1, 1], near, 1)
         c0 = back_to_cams(1) + cam_damp * z0
         u = c0 / precond
-        first = 2 * step
-        total_start(first, [lane_sum(r0 * z0), lane_sum(z0 * c0), lane_sum(c0 * u), cost_row])
-
+        hidden_start(step, [lane_sum(r0 * z0), lane_sum(z0 * c0), lane_sum(c0 * u), cost_row])
         take_cams(u, 2)
         put_points(to_points(gg[2, 0], gg[2, 1]), 0, contrib)
         collect_start(3, *pts)
+        hidden_turn(step)
         y = collect_wait(3, *pts)
         ybuf[2] = jnp.stack(y)
         w = apply_inverse([inv_b[c] for c in range(6)], y)
         wbuf[2] = jnp.stack(w)
-
-        dots = total_wait(first)
+        if last:
+            spread_start(w, *out_s)
+
+        dots = hidden_wait(step)
         resid_dot, curve, square = dots[0], dots[1], dots[2]
-        cost_o[pl.ds(step, 1), :] = jnp.broadcast_to(0.5 * dots[3], (1, LANES))
+        costs.append(0.5 * dots[3])
         alpha = resid_dot / curve
         beta = (resid_dot - 2.0 * alpha * curve + alpha * alpha * square) / resid_dot
         more = 1.0 + beta
@@ -601,8 +683,6 @@
                 + inner(w_base, hw_turn),
                 turn_sq - 2.0 * yw + inner(w_turn, hw_turn),
             ]
-        second = first + 1
-        total_start(second, rows)
         if not last:
             hess = [hess_b[c] for c in range(6)]
             inv = invert(hess, LAMBDAS[1])
@@ -620,16 +700,17 @@
             w_fix = apply_inverse(inv, y_fix)
             w_move = apply_inverse(inv, y_move)
             spread_start(w_fix + mix(1.0, w_move, -alpha, w), *out_w)
+            total_start(step, rows)
             spread_start(w, *out_2)
             spread_wait(*out_w)
             near_fix = take_points(recv_w)
             near_move = take_points(recv_w, 3)
         else:
-            spread_start(w, *out_s)
+            total_start(step, rows)
             spread_wait(*out_s)
             near = take_points(recv_s)
             eliminate(gg[2, 0], gg[2, 1], near, 2)
-        dots = total_wait(second)
+        dots = total_wait(step)
         alpha1 = dots[0] / dots[1]
         ca = alpha + alpha1 * more
         cb = -(alpha1 * alpha)
@@ -646,15 +727,25 @@
             wbuf[0] = jnp.stack(mix(1.0, w_fix, alpha1, w_move))
         else:
             for r in range(2):
-                res_o[r] = bk[0, r] + ca * bk[1, r] + cb * bk[2, r]
-            cost_o[pl.ds(2, 1), :] = jnp.broadcast_to(
-                0.5 * (dots[2] + 2.0 * alpha1 * dots[3] + alpha1 * alpha1 * dots[4]), (1, LANES)
-            )
-    upd_o[...] = upd_sum
-    step_o[...] = step_sum
-    cost_o[pl.ds(3, 5), :] = jnp.zeros((5, LANES), F32)
-    for a in range(4):
+                res_o[pl.ds(r, TILES, stride=2), :] = bk[0, r] + ca * bk[1, r] + cb * bk[2, r]
+            costs.append(0.5 * (dots[2] + 2.0 * alpha1 * dots[3] + alpha1 * alpha1 * dots[4]))
+    for p in range(2):
+        both = upd_sum[:, p, :]
+        cam_o[:, 2 * p, :] = cam_r[:, 2 * p, :] + both[:, 0:64]
+        cam_o[:, 2 * p + 1, :] = cam_r[:, 2 * p + 1, :] + both[:, 64:128]
+    pt_o[...] = pt_r[...] + step_sum
+    third = lax.broadcasted_iota(jnp.int32, (1, 3), 1)
+    cost_o[...] = jnp.where(third == 0, costs[0], jnp.where(third == 1, costs[1], costs[2]))
+    for a in range(2):
+        hidden_drain(a)
         total_drain(a)
+
+
+def hand_over(cam_i, pt_i, res_i, cost_i, cam_o, pt_o, res_o, cost_o):
+    res_o[...] = res_i[...]
+    cam_o[...] = cam_i[...]
+    pt_o[...] = pt_i[...]
+    cost_o[...] = cost_i[...]
 
 
 def body(
@@ -671,30 +762,34 @@
     cg_start,
 ):
     vmem = pl.BlockSpec(memory_space=pltpu.VMEM)
-    hbm = pl.BlockSpec(memory_space=pl.ANY)
+    hbm = pl.BlockSpec(memory_space=pltpu.HBM)
     big = (TILES, LANES)
     blk = (NBLK, LANES)
     dma = pltpu.SemaphoreType.DMA
-    upd, steps, res, costs = pl.pallas_call(
+    shapes = [
+        jax.ShapeDtypeStruct((CPAR, 4, 64), F32),
+        jax.ShapeDtypeStruct((3,) + blk, F32),
+        jax.ShapeDtypeStruct((2 * TILES, LANES), F32),
+        jax.ShapeDtypeStruct((1, 3), F32),
+    ]
+    results = pl.pallas_call(
         kernel,
-        out_shape=[
-            jax.ShapeDtypeStruct((CPAR, 2, LANES), F32),
-            jax.ShapeDtypeStruct((3,) + blk, F32),
-            jax.ShapeDtypeStruct((2,) + big, F32),
-            jax.ShapeDtypeStruct((8, LANES), F32),
-        ],
-        in_specs=[pl.BlockSpec(memory_space=pltpu.SMEM)] + [hbm] * 9,
+        out_shape=shapes,
+        in_specs=[pl.BlockSpec(memory_space=pltpu.SMEM)] + [hbm] * 11,
         out_specs=[vmem] * 4,
         scratch_shapes=[
             pltpu.VMEM((18,) + big, F32),
             pltpu.VMEM((6,) + big, F32),
             pltpu.VMEM((2,) + big, F32),
+            pltpu.VMEM((2 * TILES, LANES), F32),
             pltpu.VMEM(big, jnp.int32),
             pltpu.VMEM(big, jnp.int32),
             pltpu.VMEM((1, LANES), jnp.int32),
             pltpu.VMEM((1, LANES), jnp.int32),
             pltpu.VMEM((1, LANES), jnp.int32),
             pltpu.VMEM((CPAR, 4, 64), F32),
+            pltpu.VMEM((CPAR, 4, 64), F32),
+            pltpu.VMEM((3,) + blk, F32),
             pltpu.VMEM((18,) + big, F32),
             pltpu.VMEM((6,) + big, F32),
             pltpu.VMEM((PAD + LANES, LANES), F32),
@@ -728,12 +823,16 @@
             pltpu.VMEM((3, 3) + blk, F32),
             pltpu.VMEM((CPAR, 2, LANES), F32),
             pltpu.VMEM((CPAR, 2, LANES), F32),
-            pltpu.VMEM((4, 1, LANES), F32),
-            pltpu.VMEM((4, GX * GY, LANES), F32),
-            dma((10,)),
+            pltpu.VMEM((2, 1, LANES), F32),
+            pltpu.VMEM((2, GX * GY, LANES), F32),
+            pltpu.VMEM((2, 1, LANES), F32),
+            pltpu.VMEM((2, GX, LANES), F32),
+            pltpu.VMEM((2, 1, LANES), F32),
+            pltpu.VMEM((2, GY, LANES), F32),
+            dma((11,)),
         ]
         + [dma((8,))] * 10
-        + [dma((4,))] * 2,
+        + [dma((2,))] * 6,
         compiler_params=pltpu.CompilerParams(
             collective_id=0, has_side_effects=True, vmem_limit_bytes=62 * 1024 * 1024
         ),
@@ -741,19 +840,25 @@
         tile_points[0, 0],
         jnp.transpose(jac_cam[0, 0], (1, 0, 2)),
         jnp.transpose(jac_pt[0, 0], (1, 0, 2)),
-        resid0[0, 0],
+        resid0.reshape(2 * TILES, LANES),
         obs_camera[0, 0],
         obs_point[0, 0],
         obs_count[0],
         tile_camera[0],
         tile_points[0],
         jnp.transpose(cg_start[0, 0], (1, 0, 2)),
+        jnp.transpose(cam_params[0, 0], (1, 0, 2)),
+        jnp.transpose(pt_params[0, 0], (1, 0, 2)),
     )
-    moved = jnp.transpose(upd.reshape(CPAR, 2, 2, 64), (1, 2, 0, 3)).reshape(4, CPAR, 64)
-    cam_out = cam_params + moved[None, None]
-    pt_out = pt_params + jnp.transpose(steps, (1, 0, 2))[None, None]
-    res_out = jnp.transpose(res, (1, 0, 2))[None, None]
-    return cam_out, pt_out, res_out, costs[:3, 0]
+    cam, pt, res, costs = pl.pallas_call(
+        hand_over,
+        out_shape=shapes,
+        in_specs=[vmem] * 4,
+        out_specs=[vmem] * 4,
+    )(*results)
+    cam_out = jnp.transpose(cam, (1, 0, 2))[None, None]
+    pt_out = jnp.transpose(pt, (1, 0, 2))[None, None]
+    return cam_out, pt_out, res.reshape(1, 1, TILES, 2, LANES), costs.reshape(3)
 
 
 def solution(mesh):

time: 91 us -> 85.1 us (0.935)
  local copies, waits for them, and re-layouts: 3.76 us -> 0 us
  other arithmetic: 1.96 us -> 0 us
    add x2 -> x0, other arithmetic: 1.96 us -> none  [the longest x1 1.35 us: body(): pt_out = pt_params + jnp.transpose(steps, (1, 0, 2))[None, None]]
    unnamed x5 -> x0, local copies, waits for them, and re-layouts: 1.67 us -> none
    slice x1 -> x0, local copies, waits for them, and re-layouts: 1.3 us -> none  [body(): return (cam_out, pt_out, res_out, costs[:3, 0])]
    pallas_call x1 -> x2, Pallas kernels: 84.3 us -> 84.3 us  [the longest x1 82.7 us: body(): pl.pallas_call(kernel, out_shape=shapes, in_specs=[pl.BlockSpec(memory_sp...]
where the time goes in v4:
time: 85.1 us; the launch traced here: 85 us
  Pallas kernels  84.3 us (99%)
    pallas_call x1, Pallas kernels, body(): pl.pallas_call(kernel, out_shape=shapes, in_specs=[pl.BlockSpec(memory_sp...  82.7 us

profile of v4, /device:TPU:1, one launch (start us, length us, event | category | flops | bytes accessed | tf_op | source)
XLA Modules:
  0.0 85.0 jit_solution(18218680199984415022)
XLA Ops:
  0.6 82.7 %shard_map.138 = (f32[9,4,64]{2,1,0:T(4,128)}, f32[3,16,128]{2,1,0:T(8,128)}, f32[256,128]{1,0:T(8,128)}, f32[1,3]{1,0:T(1,128)}) custom-call(s32[128]{0:T(128)} %bitcast.38, f32[18,128,128]{2,1,0:T(8,128)} %bitcast.30, f32[6,128,128]{2,1,0:T(8,128)} %bitcast.31, f32[256,128]{1,0:T(8,128)} %bitcast.32, s32[128,128]{1,0:T(8,128)} %bitcast.33, ...), custom_call_target="tpu_custom_call" | custom-call | tf_op jit(solution)/shard_map/pallas_call | solution.py:775
  83.4 1.6 %shard_map.139 = (f32[9,4,64]{2,1,0:T(4,128)}, f32[3,16,128]{2,1,0:T(8,128)}, f32[256,128]{1,0:T(8,128)}, f32[1,3]{1,0:T(1,128)}) custom-call(f32[9,4,64]{2,1,0:T(4,128)} %get-tuple-element.12.cam_i, f32[3,16,128]{2,1,0:T(8,128)} %get-tuple-element.13.pt_i, f32[256,128]{1,0:T(8,128)} %get-tuple-element.14.res_i, f32[1,3]{1,0:T(1,128)} %get-tuple-element.15.cost_i), custom_call_target="tpu_custom_call" | custom-call | tf_op jit(solution)/shard_map/pallas_call | solution.py:853

commit v5 on v4

--- a/solution.py
+++ b/solution.py
@@ -159,6 +159,7 @@
     hit_p,
     hit_c,
     pair_m,
+    valid_m,
     idx_c,
     onehot,
     table,
@@ -167,6 +168,8 @@
     mv,
     contrib,
     recv_c,
+    contrib_h,
+    recv_h,
     contrib_y,
     recv_y,
     wsrc,
@@ -188,8 +191,11 @@
     py_src,
     py_dst,
     in_sem,
+    row_s,
     cs_sem,
     cr_sem,
+    hs_sem,
+    hr_sem,
     ys_sem,
     yr_sem,
     ss_sem,
@@ -253,17 +259,17 @@
         @pl.when(jnp.logical_not(here[n]))
         def _(r=r, n=n):
             recv_c[r] = jnp.zeros_like(recv_c[r])
-            recv_s[n] = jnp.zeros_like(recv_s[n])
-            recv_w[n] = jnp.zeros_like(recv_w[n])
-            recv_2[n] = jnp.zeros_like(recv_2[n])
+            recv_h[r] = jnp.zeros_like(recv_h[r])
             recv_y[r] = jnp.zeros_like(recv_y[r])
+            for buf in (recv_s, recv_w, recv_2):
+                per = buf.shape[0] // 9
+                buf[n * per : (n + 1) * per, :] = jnp.zeros((per, LANES), F32)
 
     barrier = pltpu.get_barrier_semaphore()
-    to_all(
-        lambda dx, dy: pl.semaphore_signal(
-            barrier, inc=1, device_id=at(dx, dy), device_id_type=MESH
-        )
-    )
+    greeted = [(-1, -1), (-1, 1), (1, -1), (1, 1)]
+    greeted += [(0, d) for d in range(1, GY)] + [(d, 0) for d in range(1, GX)]
+    for dx, dy in greeted:
+        pl.semaphore_signal(barrier, inc=1, device_id=at(dx, dy), device_id_type=MESH)
 
     seg_t[0:PAD, :] = jnp.full((PAD, LANES), -1.0, F32)
     for k in range(CPAR):
@@ -305,7 +311,7 @@
             for k in range(count)
         ]
 
-    def put_points(values, first, dest):
+    def put_points(values, dest):
         sums = jnp.concatenate([v * hit_p[...] for v in summed(values, 0)], axis=1)
         high = sums.astype(BF16)
         rest = sums - high.astype(F32)
@@ -314,10 +320,8 @@
         parts = jnp.concatenate([high, mid, low], axis=0)
         out = jnp.dot(onehot[...], parts, preferred_element_type=F32)
         for n in range(9):
-            for m in range(3):
-                dest[n, first + m] = out[
-                    n * NBLK : (n + 1) * NBLK, m * LANES : (m + 1) * LANES
-                ]
+            for m in range(len(values)):
+                dest[n, m] = out[n * NBLK : (n + 1) * NBLK, m * LANES : (m + 1) * LANES]
 
     def put_cams(values):
         for k, sums in enumerate(summed(values, 1)):
@@ -346,8 +350,8 @@
                 got = pick(src, idx)
                 e0 = e0 + jc[k, where, :] * got
                 e1 = e1 + jc[CPAR + k, where, :] * got
-            gg[b, 0, where, :] = e0
-            gg[b, 1, where, :] = e1
+            gg[b, 0, where, :] = e0 * valid_m[where, :]
+            gg[b, 1, where, :] = e1 * valid_m[where, :]
             return carry
 
         lax.fori_loop(0, TILES // rows, one, 0)
@@ -390,15 +394,17 @@
         return total
 
     pts = (contrib, recv_c, cs_sem, cr_sem)
+    pts_h = (contrib_h, recv_h, hs_sem, hr_sem)
     pts_y = (contrib_y, recv_y, ys_sem, yr_sem)
     out_s = (wsrc, recv_s, ss_sem, sr_sem)
     out_w = (wsrc_w, recv_w, ws_sem, wr_sem)
     out_2 = (wsrc_2, recv_2, s2_sem, r2_sem)
 
     def spread_start(values, src, dst, send_sem, recv_sem):
+        per = src.shape[0]
         for m, v in enumerate(values):
-            src[m] = v
-            dst[4, m] = v
+            src[m * NBLK : (m + 1) * NBLK, :] = v
+            dst[4 * per + m * NBLK : 4 * per + (m + 1) * NBLK, :] = v
         for r, n in ORDER:
             a, b = divmod(n, 3)
 
@@ -406,7 +412,7 @@
             def _(r=r, n=n, a=a, b=b):
                 pltpu.make_async_remote_copy(
                     src_ref=src,
-                    dst_ref=dst.at[8 - n],
+                    dst_ref=dst.at[pl.ds((8 - n) * per, per)],
                     send_sem=send_sem.at[r],
                     recv_sem=recv_sem.at[r],
                     device_id=at(a - 1, b - 1),
@@ -414,25 +420,28 @@
                 ).start()
 
     def spread_wait(src, dst, send_sem, recv_sem):
+        per = src.shape[0]
         for sem, flip in ((recv_sem, True), (send_sem, False)):
             for r, n in enumerate(OTHERS):
 
                 @pl.when(here[8 - n] if flip else here[n])
                 def _(r=r, n=n, sem=sem):
-                    pltpu.make_async_copy(src, dst.at[8 - n], sem.at[r]).wait()
+                    pltpu.make_async_copy(
+                        src, dst.at[pl.ds((8 - n) * per, per)], sem.at[r]
+                    ).wait()
 
     def take_points(src, first=0):
+        per = src.shape[0] // 9
+
         def one(chunk, carry):
-            for i in range(8):
-                t = chunk * 8 + i
-                slot = slot_s[t]
-                n = slot >> 4
-                q = slot & 15
+            for i in range(16):
+                t = chunk * 16 + i
+                row = row_s[0 if per == 3 * NBLK else 1, t] + first * NBLK
                 for m in range(3):
-                    table[m, pl.ds(t, 1), :] = src[n, first + m, pl.ds(q, 1), :]
+                    table[m, pl.ds(t, 1), :] = src[pl.ds(row + m * NBLK, 1), :]
             return carry
 
-        lax.fori_loop(0, TILES // 8, one, 0)
+        lax.fori_loop(0, TILES // 16, one, 0)
         return [pick(table[m], obs_pt[...]) for m in range(3)]
 
     def eliminate(e0, e1, near, b):
@@ -529,23 +538,23 @@
     hot = jnp.where(slot_row == tpts_r[...], 1.0, 0.0).astype(BF16)
     for i in range(3):
         onehot[:, i * TILES : (i + 1) * TILES] = hot
+    valid_m[...] = jnp.where(lane < column(count_r[...]).astype(jnp.int32), 1.0, 0.0)
+    valid = valid_m[...]
     tcam = column(tcam_r[...]).astype(jnp.int32)
     parity = tcam & 1
     pair = tcam >> 1
     pair_m[...] = pair
     idx_c[...] = parity * 64 + obs_cam[...]
 
-    valid = jnp.where(lane < column(count_r[...]).astype(jnp.int32), 1.0, 0.0)
     for k in range(2):
         rs[k] = rs_in[pl.ds(k, TILES, stride=2), :] * valid
     for k in range(6):
         jp[k] = jp[k] * valid
         jpt[k] = sorted_t(jp[k], 0)
-    for k in range(18):
-        jc[k] = jc[k] * valid
     square = [jpt[i] * jpt[j] + jpt[3 + i] * jpt[3 + j] for i, j in PAIRS]
-    put_points(square[0:3], 0, contrib)
-    put_points(square[3:6], 3, contrib)
+    put_points(square, contrib_h)
+    pl.semaphore_wait(barrier, len(greeted))
+    collect_start(6, *pts_h)
 
     start = jnp.concatenate(
         [
@@ -557,23 +566,33 @@
     take_cams(start, 0)
     for k in range(2):
         mv[k] = rs[k] + gg[0, k]
-    put_points(to_points(mv[0], mv[1]), 6, contrib)
-    pl.semaphore_wait(barrier, GX * GY - 1)
-    collect_start(9, *pts)
-    put_points(to_points(gg[0, 0], gg[0, 1]), 0, contrib_y)
+    put_points(to_points(mv[0], mv[1]), contrib)
+    collect_start(3, *pts)
+    put_points(to_points(gg[0, 0], gg[0, 1]), contrib_y)
     collect_start(3, *pts_y)
+    def rows_of(t, carry):
+        slot = slot_s[t]
+        n, q = slot >> 4, slot & 15
+        row_s[0, t] = n * (3 * NBLK) + q
+        row_s[1, t] = n * (6 * NBLK) + q
+        return carry
+
+    lax.fori_loop(0, TILES, rows_of, 0)
     found = order(1, obs_cam[...], lane & 63)
     mine = found & ((lane >> 6) == parity)
     hit_c[0] = jnp.where(mine & (pair == 0), 1.0, 0.0)
     hit_c[1] = jnp.where(mine & (pair == 1), 1.0, 0.0)
     for k in range(18):
-        jct[k] = sorted_t(jc[k], 1)
+        jct[k] = sorted_t(jc[k] * valid, 1)
     diag = put_cams([jct[k] * jct[k] + jct[CPAR + k] * jct[CPAR + k] for k in range(CPAR)])
     cost_row = lane_sum(rs[...] * rs[...])
-    owned = collect_wait(9, *pts)
+    hess = collect_wait(6, *pts_h)
     for c in range(6):
-        hess_b[c] = owned[c]
-    ybuf[0] = jnp.stack(owned[6:9])
+        hess_b[c] = hess[c]
+    inv = invert(hess, LAMBDAS[0])
+    for c in range(6):
+        inv_b[0, c] = inv[c]
+    ybuf[0] = jnp.stack(collect_wait(3, *pts))
 
     costs = []
     update = start
@@ -597,12 +616,12 @@
     def mix(p, u, q, v):
         return [p * u[m] + q * v[m] for m in range(3)]
 
-    inv = invert([hess_b[c] for c in range(6)], LAMBDAS[0])
-    for c in range(6):
-        inv_b[c] = inv[c]
     w0 = apply_inverse(inv, three(ybuf, 0))
     wbuf[0] = jnp.stack(w0)
     spread_start(w0, *out_s)
+    inv = invert(hess, LAMBDAS[1])
+    for c in range(6):
+        inv_b[1, c] = inv[c]
     spread_wait(*out_s)
     near = take_points(recv_s)
 
@@ -617,7 +636,7 @@
         z0 = r0 / precond
 
         take_cams(z0, 1)
-        put_points(to_points(gg[1, 0], gg[1, 1]), 0, contrib)
+        put_points(to_points(gg[1, 0], gg[1, 1]), contrib)
         collect_start(3, *pts)
         if last:
             spread_wait(*out_2)
@@ -630,7 +649,7 @@
             cost_row = lane_sum(rs[...] * rs[...])
         y = collect_wait(3, *pts)
         ybuf[1] = jnp.stack(y)
-        w = apply_inverse([inv_b[c] for c in range(6)], y)
+        w = apply_inverse([inv_b[step, c] for c in range(6)], y)
         wbuf[1] = jnp.stack(w)
         spread_start(w, *out_s)
         spread_wait(*out_s)
@@ -640,15 +659,23 @@
         u = c0 / precond
         hidden_start(step, [lane_sum(r0 * z0), lane_sum(z0 * c0), lane_sum(c0 * u), cost_row])
         take_cams(u, 2)
-        put_points(to_points(gg[2, 0], gg[2, 1]), 0, contrib)
+        put_points(to_points(gg[2, 0], gg[2, 1]), contrib)
         collect_start(3, *pts)
         hidden_turn(step)
         y = collect_wait(3, *pts)
         ybuf[2] = jnp.stack(y)
-        w = apply_inverse([inv_b[c] for c in range(6)], y)
+        w = apply_inverse([inv_b[step, c] for c in range(6)], y)
         wbuf[2] = jnp.stack(w)
         if last:
             spread_start(w, *out_s)
+        else:
+            scale = [damping * (hess[c] + 1.0) for c in (0, 3, 5)]
+            y_start = collect_wait(3, *pts_y)
+            held = []
+            for b in range(3):
+                held.append([scale[m] * wbuf[b, m] + ybuf[b, m] for m in range(3)])
+            held[0] = [scale[m] * wbuf[0, m] + y_start[m] for m in range(3)]
+            moved = [apply_inverse([inv_b[1, c] for c in range(6)], y) for y in held]
 
         dots = hidden_wait(step)
         resid_dot, curve, square = dots[0], dots[1], dots[2]
@@ -658,6 +685,12 @@
         more = 1.0 + beta
         z1 = (r0 - alpha * c0) / precond
         d1 = z1 + beta * z0
+        if not last:
+            y_fix = mix(1.0, held[0], alpha, held[1])
+            y_move = mix(more, held[1], -alpha, held[2])
+            w_fix = mix(1.0, moved[0], alpha, moved[1])
+            w_move = mix(more, moved[1], -alpha, moved[2])
+            spread_start(w_fix + mix(1.0, w_move, -alpha, w), *out_w)
         turn = [more * gg[1, r] - alpha * gg[2, r] for r in range(2)]
         y_turn = mix(more, three(ybuf, 1), -alpha, three(ybuf, 2))
         w_turn = mix(more, three(wbuf, 1), -alpha, three(wbuf, 2))
@@ -683,30 +716,13 @@
                 + inner(w_base, hw_turn),
                 turn_sq - 2.0 * yw + inner(w_turn, hw_turn),
             ]
+        total_start(step, rows)
         if not last:
-            hess = [hess_b[c] for c in range(6)]
-            inv = invert(hess, LAMBDAS[1])
-            for c in range(6):
-                inv_b[c] = inv[c]
-            scale = [damping * (hess[c] + 1.0) for c in (0, 3, 5)]
-            held = []
-            for b in range(3):
-                held.append([scale[m] * wbuf[b, m] + ybuf[b, m] for m in range(3)])
-            y_start = collect_wait(3, *pts_y)
-            y_fix = [
-                scale[m] * wbuf[0, m] + y_start[m] + alpha * held[1][m] for m in range(3)
-            ]
-            y_move = mix(more, held[1], -alpha, held[2])
-            w_fix = apply_inverse(inv, y_fix)
-            w_move = apply_inverse(inv, y_move)
-            spread_start(w_fix + mix(1.0, w_move, -alpha, w), *out_w)
-            total_start(step, rows)
             spread_start(w, *out_2)
             spread_wait(*out_w)
             near_fix = take_points(recv_w)
             near_move = take_points(recv_w, 3)
         else:
-            total_start(step, rows)
             spread_wait(*out_s)
             near = take_points(recv_s)
             eliminate(gg[2, 0], gg[2, 1], near, 2)
@@ -801,24 +817,27 @@
             pltpu.VMEM(big, F32),
             pltpu.VMEM((2,) + big, F32),
             pltpu.VMEM(big, jnp.int32),
+            pltpu.VMEM(big, F32),
             pltpu.VMEM(big, jnp.int32),
             pltpu.VMEM((SLOTS, 3 * TILES), BF16),
             pltpu.VMEM((3,) + big, F32),
             pltpu.VMEM((3, 2) + big, F32),
             pltpu.VMEM((3, 2) + big, F32),
             pltpu.VMEM((2,) + big, F32),
-            pltpu.VMEM((9, 9) + blk, F32),
-            pltpu.VMEM((8, 9) + blk, F32),
             pltpu.VMEM((9, 3) + blk, F32),
             pltpu.VMEM((8, 3) + blk, F32),
-            pltpu.VMEM((3,) + blk, F32),
+            pltpu.VMEM((9, 6) + blk, F32),
+            pltpu.VMEM((8, 6) + blk, F32),
             pltpu.VMEM((9, 3) + blk, F32),
+            pltpu.VMEM((8, 3) + blk, F32),
+            pltpu.VMEM((3 * NBLK, LANES), F32),
+            pltpu.VMEM((27 * NBLK, LANES), F32),
+            pltpu.VMEM((6 * NBLK, LANES), F32),
+            pltpu.VMEM((54 * NBLK, LANES), F32),
+            pltpu.VMEM((3 * NBLK, LANES), F32),
+            pltpu.VMEM((27 * NBLK, LANES), F32),
             pltpu.VMEM((6,) + blk, F32),
-            pltpu.VMEM((9, 6) + blk, F32),
-            pltpu.VMEM((3,) + blk, F32),
-            pltpu.VMEM((9, 3) + blk, F32),
-            pltpu.VMEM((6,) + blk, F32),
-            pltpu.VMEM((6,) + blk, F32),
+            pltpu.VMEM((2, 6) + blk, F32),
             pltpu.VMEM((3, 3) + blk, F32),
             pltpu.VMEM((3, 3) + blk, F32),
             pltpu.VMEM((CPAR, 2, LANES), F32),
@@ -830,8 +849,9 @@
             pltpu.VMEM((2, 1, LANES), F32),
             pltpu.VMEM((2, GY, LANES), F32),
             dma((11,)),
+            pltpu.SMEM((2, LANES), jnp.int32),
         ]
-        + [dma((8,))] * 10
+        + [dma((8,))] * 12
         + [dma((2,))] * 6,
         compiler_params=pltpu.CompilerParams(
             collective_id=0, has_side_effects=True, vmem_limit_bytes=62 * 1024 * 1024

time: 85.1 us -> 82.3 us (0.967)
  Pallas kernels: 84.3 us -> 81.5 us
    pallas_call x1, Pallas kernels: 82.7 us -> 79.9 us  [body(): pl.pallas_call(kernel, out_shape=shapes, in_specs=[pl.BlockSpec(memory_sp...]
where the time goes in v5:
time: 82.3 us; the launch traced here: 82.2 us
  Pallas kernels  81.5 us (99%)
    pallas_call x1, Pallas kernels, body(): pl.pallas_call(kernel, out_shape=shapes, in_specs=[pl.BlockSpec(memory_sp...  79.9 us

profile of v5, /device:TPU:1, one launch (start us, length us, event | category | flops | bytes accessed | tf_op | source)
XLA Modules:
  0.0 82.2 jit_solution(2842342604842905644)
XLA Ops:
  0.6 79.9 %shard_map.138 = (f32[9,4,64]{2,1,0:T(4,128)}, f32[3,16,128]{2,1,0:T(8,128)}, f32[256,128]{1,0:T(8,128)}, f32[1,3]{1,0:T(1,128)}) custom-call(s32[128]{0:T(128)} %bitcast.38, f32[18,128,128]{2,1,0:T(8,128)} %bitcast.30, f32[6,128,128]{2,1,0:T(8,128)} %bitcast.31, f32[256,128]{1,0:T(8,128)} %bitcast.32, s32[128,128]{1,0:T(8,128)} %bitcast.33, ...), custom_call_target="tpu_custom_call" | custom-call | tf_op jit(solution)/shard_map/pallas_call | solution.py:791
  80.6 1.6 %shard_map.139 = (f32[9,4,64]{2,1,0:T(4,128)}, f32[3,16,128]{2,1,0:T(8,128)}, f32[256,128]{1,0:T(8,128)}, f32[1,3]{1,0:T(1,128)}) custom-call(f32[9,4,64]{2,1,0:T(4,128)} %get-tuple-element.12.cam_i, f32[3,16,128]{2,1,0:T(8,128)} %get-tuple-element.13.pt_i, f32[256,128]{1,0:T(8,128)} %get-tuple-element.14.res_i, f32[1,3]{1,0:T(1,128)} %get-tuple-element.15.cost_i), custom_call_target="tpu_custom_call" | custom-call | tf_op jit(solution)/shard_map/pallas_call | solution.py:873

commit v6 on v5

--- a/solution.py
+++ b/solution.py
@@ -453,15 +453,15 @@
         return put_cams([jct[k] * t0 + jct[CPAR + k] * t1 for k in range(CPAR)])
 
     def lane_row(rows):
-        held = jnp.concatenate(rows + [jnp.zeros((8 - len(rows), LANES), F32)], axis=0)
+        held = jnp.concatenate(rows + [jnp.zeros((16 - len(rows), LANES), F32)], axis=0)
         sums = jnp.sum(held, axis=1, keepdims=True)
-        own = lax.broadcasted_iota(jnp.int32, (8, LANES), 0)
-        return jnp.sum(jnp.where(lane_ids(8) == own, sums, 0.0), axis=0, keepdims=True)
-
-    def apart(row):
+        own = lax.broadcasted_iota(jnp.int32, (16, LANES), 0)
+        return jnp.sum(jnp.where(lane_ids(16) == own, sums, 0.0), axis=0, keepdims=True)
+
+    def apart(row, count):
         lane1 = lane_ids(1)
         return [
-            jnp.sum(jnp.where(lane1 == i, row, 0.0), axis=1, keepdims=True) for i in range(8)
+            jnp.sum(jnp.where(lane1 == i, row, 0.0), axis=1, keepdims=True) for i in range(count)
         ]
 
     def pass_start(src, dst, spot, peers, send_sem, recv_sem):
@@ -494,7 +494,7 @@
     def hidden_wait(a):
         rest = py_dst.at[a, pl.ds(0, GY - 1)]
         pltpu.make_async_copy(rest, rest, pyr_sem.at[a]).wait()
-        return apart(jnp.sum(py_dst[a], axis=0, keepdims=True))
+        return apart(jnp.sum(py_dst[a], axis=0, keepdims=True), 3)
 
     def hidden_drain(a):
         rest = px_dst.at[a, pl.ds(0, GX - 1)]
@@ -523,7 +523,7 @@
         pltpu.make_async_copy(
             arx.at[a, pl.ds(0, 127)], arx.at[a, pl.ds(0, 127)], ar_sem.at[a]
         ).wait()
-        return apart(jnp.sum(arx[a], axis=0, keepdims=True))
+        return apart(jnp.sum(arx[a], axis=0, keepdims=True), 9)
 
     def total_drain(a):
         pltpu.make_async_copy(
@@ -652,16 +652,64 @@
         w = apply_inverse([inv_b[step, c] for c in range(6)], y)
         wbuf[1] = jnp.stack(w)
         spread_start(w, *out_s)
+        g1_sq = lane_sum(gg[1, 0] * gg[1, 0] + gg[1, 1] * gg[1, 1])
+        yw1 = inner(y, w)
+        hidden_start(
+            step,
+            [lane_sum(r0 * z0), g1_sq - yw1 + lane_sum(cam_damp * (z0 * z0)), cost_row],
+        )
         spread_wait(*out_s)
         near = take_points(recv_s)
         eliminate(gg[1, 0], gg[1, 1], near, 1)
         c0 = back_to_cams(1) + cam_damp * z0
+        hidden_turn(step)
         u = c0 / precond
-        hidden_start(step, [lane_sum(r0 * z0), lane_sum(z0 * c0), lane_sum(c0 * u), cost_row])
+
         take_cams(u, 2)
         put_points(to_points(gg[2, 0], gg[2, 1]), contrib)
         collect_start(3, *pts)
-        hidden_turn(step)
+
+        dots = hidden_wait(step)
+        resid_dot, curve = dots[0], dots[1]
+        costs.append(0.5 * dots[2])
+        alpha = resid_dot / curve
+        r1 = r0 - alpha * c0
+        z1 = r1 / precond
+        turn = [gg[1, r] - alpha * gg[2, r] for r in range(2)]
+        turn_sq = lane_sum(turn[0] * turn[0] + turn[1] * turn[1])
+        turn_damp = lane_sum(cam_damp * (z1 * z1))
+        rows = [lane_sum(r1 * z1), lane_sum(z1 * c0)]
+        if last:
+            base = [mv[r] + alpha * gg[1, r] for r in range(2)]
+            y_base = mix(1.0, three(ybuf, 0), alpha, three(ybuf, 1))
+            w_base = mix(1.0, three(wbuf, 0), alpha, three(wbuf, 1))
+            hw_base = weighted(w_base)
+            w1 = three(wbuf, 1)
+            hw_one = weighted(w1)
+            y1 = three(ybuf, 1)
+            rows += [
+                lane_sum(base[0] * base[0] + base[1] * base[1])
+                - 2.0 * inner(y_base, w_base)
+                + inner(w_base, hw_base),
+                lane_sum(base[0] * gg[1, 0] + base[1] * gg[1, 1])
+                - inner(y_base, w1)
+                - inner(y1, w_base)
+                + inner(w_base, hw_one),
+                g1_sq - 2.0 * yw1 + inner(w1, hw_one),
+            ]
+            base_turn = lane_sum(base[0] * turn[0] + base[1] * turn[1])
+            one_turn = lane_sum(gg[1, 0] * turn[0] + gg[1, 1] * turn[1])
+        else:
+            scale = [damping * (hess[c] + 1.0) for c in (0, 3, 5)]
+            y_start = collect_wait(3, *pts_y)
+            inv_next = [inv_b[1, c] for c in range(6)]
+            held = [
+                [scale[m] * wbuf[0, m] + y_start[m] for m in range(3)],
+                [scale[m] * wbuf[1, m] + ybuf[1, m] for m in range(3)],
+            ]
+            ahead = [apply_inverse(inv_next, v) for v in held]
+            spread_start(mix(1.0, ahead[0], alpha, ahead[1]) + ahead[1], *out_w)
+
         y = collect_wait(3, *pts)
         ybuf[2] = jnp.stack(y)
         w = apply_inverse([inv_b[step, c] for c in range(6)], y)
@@ -669,51 +717,21 @@
         if last:
             spread_start(w, *out_s)
         else:
-            scale = [damping * (hess[c] + 1.0) for c in (0, 3, 5)]
-            y_start = collect_wait(3, *pts_y)
-            held = []
-            for b in range(3):
-                held.append([scale[m] * wbuf[b, m] + ybuf[b, m] for m in range(3)])
-            held[0] = [scale[m] * wbuf[0, m] + y_start[m] for m in range(3)]
-            moved = [apply_inverse([inv_b[1, c] for c in range(6)], y) for y in held]
-
-        dots = hidden_wait(step)
-        resid_dot, curve, square = dots[0], dots[1], dots[2]
-        costs.append(0.5 * dots[3])
-        alpha = resid_dot / curve
-        beta = (resid_dot - 2.0 * alpha * curve + alpha * alpha * square) / resid_dot
-        more = 1.0 + beta
-        z1 = (r0 - alpha * c0) / precond
-        d1 = z1 + beta * z0
-        if not last:
-            y_fix = mix(1.0, held[0], alpha, held[1])
-            y_move = mix(more, held[1], -alpha, held[2])
-            w_fix = mix(1.0, moved[0], alpha, moved[1])
-            w_move = mix(more, moved[1], -alpha, moved[2])
-            spread_start(w_fix + mix(1.0, w_move, -alpha, w), *out_w)
-        turn = [more * gg[1, r] - alpha * gg[2, r] for r in range(2)]
-        y_turn = mix(more, three(ybuf, 1), -alpha, three(ybuf, 2))
-        w_turn = mix(more, three(wbuf, 1), -alpha, three(wbuf, 2))
-        turn_sq = lane_sum(turn[0] * turn[0] + turn[1] * turn[1])
+            held.append([scale[m] * w[m] + y[m] for m in range(3)])
+            ahead.append(apply_inverse(inv_next, held[2]))
+            spread_start([-alpha * (ahead[2][m] + w[m]) for m in range(3)], *out_s)
+        y_turn = mix(1.0, three(ybuf, 1), -alpha, y)
+        w_turn = mix(1.0, three(wbuf, 1), -alpha, w)
         yw = inner(y_turn, w_turn)
-        rows = [
-            lane_sum((r0 - alpha * c0) * z1),
-            turn_sq - yw + lane_sum(cam_damp * (d1 * d1)),
-        ]
+        rows.append(turn_sq - yw + turn_damp)
         if last:
-            base = [mv[r] + alpha * gg[1, r] for r in range(2)]
-            y_base = mix(1.0, three(ybuf, 0), alpha, three(ybuf, 1))
-            w_base = mix(1.0, three(wbuf, 0), alpha, three(wbuf, 1))
-            hw_base = weighted(w_base)
             hw_turn = weighted(w_turn)
             rows += [
-                lane_sum(base[0] * base[0] + base[1] * base[1])
-                - 2.0 * inner(y_base, w_base)
-                + inner(w_base, hw_base),
-                lane_sum(base[0] * turn[0] + base[1] * turn[1])
+                base_turn
                 - inner(y_base, w_turn)
                 - inner(y_turn, w_base)
                 + inner(w_base, hw_turn),
+                one_turn - inner(y1, w_turn) - inner(y_turn, w1) + inner(w1, hw_turn),
                 turn_sq - 2.0 * yw + inner(w_turn, hw_turn),
             ]
         total_start(step, rows)
@@ -721,30 +739,51 @@
             spread_start(w, *out_2)
             spread_wait(*out_w)
             near_fix = take_points(recv_w)
-            near_move = take_points(recv_w, 3)
+            near_one = take_points(recv_w, 3)
+            spread_wait(*out_s)
+            near_move = take_points(recv_s)
         else:
             spread_wait(*out_s)
             near = take_points(recv_s)
             eliminate(gg[2, 0], gg[2, 1], near, 2)
         dots = total_wait(step)
-        alpha1 = dots[0] / dots[1]
+        fresh, cross = dots[0], dots[1]
+        beta = fresh / resid_dot
+        more = 1.0 + beta
+        curve1 = dots[5 if last else 2] + 2.0 * beta * cross + beta * beta * curve
+        alpha1 = fresh / curve1
         ca = alpha + alpha1 * more
         cb = -(alpha1 * alpha)
-        update = update + alpha * z0 + alpha1 * d1
+        update = update + alpha * z0 + alpha1 * (z1 + beta * z0)
         upd_sum = upd_sum + update
         step_sum = step_sum - (wbuf[0] + ca * wbuf[1] + cb * wbuf[2])
         if not last:
-            near = [near_fix[m] + alpha1 * near_move[m] for m in range(3)]
+            step1 = alpha1 * more
+            near = [
+                near_fix[m] + step1 * near_one[m] + alpha1 * near_move[m] for m in range(3)
+            ]
             for r in range(2):
                 rs[r] = bk[0, r] + ca * bk[1, r] + cb * gg[2, r]
                 mv[r] = gg[0, r] + ca * gg[1, r] + cb * gg[2, r]
             eliminate(rs[0] + mv[0], rs[1] + mv[1], near, 0)
-            ybuf[0] = jnp.stack(mix(1.0, y_fix, alpha1, y_move))
-            wbuf[0] = jnp.stack(mix(1.0, w_fix, alpha1, w_move))
+            ybuf[0] = jnp.stack([held[0][m] + ca * held[1][m] + cb * held[2][m] for m in range(3)])
+            wbuf[0] = jnp.stack(
+                [ahead[0][m] + ca * ahead[1][m] + cb * ahead[2][m] for m in range(3)]
+            )
         else:
             for r in range(2):
                 res_o[pl.ds(r, TILES, stride=2), :] = bk[0, r] + ca * bk[1, r] + cb * bk[2, r]
-            costs.append(0.5 * (dots[2] + 2.0 * alpha1 * dots[3] + alpha1 * alpha1 * dots[4]))
+            base_sq, base_one, one_sq = dots[2], dots[3], dots[4]
+            base_dot, one_dot, turn_dot = dots[6], dots[7], dots[8]
+            square = turn_dot + 2.0 * beta * one_dot + beta * beta * one_sq
+            costs.append(
+                0.5
+                * (
+                    base_sq
+                    + 2.0 * alpha1 * (base_dot + beta * base_one)
+                    + alpha1 * alpha1 * square
+                )
+            )
     for p in range(2):
         both = upd_sum[:, p, :]
         cam_o[:, 2 * p, :] = cam_r[:, 2 * p, :] + both[:, 0:64]

time: 82.3 us -> 79.7 us (0.968)
  Pallas kernels: 81.5 us -> 78.9 us
    pallas_call x1, Pallas kernels: 79.9 us -> 77.3 us  [body(): pl.pallas_call(kernel, out_shape=shapes, in_specs=[pl.BlockSpec(memory_sp...]
where the time goes in v6:
time: 79.7 us; the launch traced here: 79.6 us
  Pallas kernels  78.9 us (99%)
    pallas_call x1, Pallas kernels, body(): pl.pallas_call(kernel, out_shape=shapes, in_specs=[pl.BlockSpec(memory_sp...  77.3 us
    pallas_call x1, Pallas kernels, body(): pl.pallas_call(hand_over, out_shape=shapes, in_specs=[vmem] * 4, out_spec...  1.62 us

profile of v6, /device:TPU:1, one launch (start us, length us, event | category | flops | bytes accessed | tf_op | source)
XLA Modules:
  0.0 79.6 jit_solution(4199856854147879750)
XLA Ops:
  0.6 77.3 %shard_map.138 = (f32[9,4,64]{2,1,0:T(4,128)}, f32[3,16,128]{2,1,0:T(8,128)}, f32[256,128]{1,0:T(8,128)}, f32[1,3]{1,0:T(1,128)}) custom-call(s32[128]{0:T(128)} %bitcast.38, f32[18,128,128]{2,1,0:T(8,128)} %bitcast.30, f32[6,128,128]{2,1,0:T(8,128)} %bitcast.31, f32[256,128]{1,0:T(8,128)} %bitcast.32, s32[128,128]{1,0:T(8,128)} %bitcast.33, ...), custom_call_target="tpu_custom_call" | custom-call | tf_op jit(solution)/shard_map/pallas_call | solution.py:830
  78.0 1.6 %shard_map.139 = (f32[9,4,64]{2,1,0:T(4,128)}, f32[3,16,128]{2,1,0:T(8,128)}, f32[256,128]{1,0:T(8,128)}, f32[1,3]{1,0:T(1,128)}) custom-call(f32[9,4,64]{2,1,0:T(4,128)} %get-tuple-element.12.cam_i, f32[3,16,128]{2,1,0:T(8,128)} %get-tuple-element.13.pt_i, f32[256,128]{1,0:T(8,128)} %get-tuple-element.14.res_i, f32[1,3]{1,0:T(1,128)} %get-tuple-element.15.cost_i), custom_call_target="tpu_custom_call" | custom-call | tf_op jit(solution)/shard_map/pallas_call | solution.py:912

commit v7 on v6

--- a/solution.py
+++ b/solution.py
@@ -224,16 +224,18 @@
         x, y = me_x + (a - 1), me_y + (b - 1)
         here[n] = (x >= 0) & (x < GX) & (y >= 0) & (y < GY)
 
+    columns = {dx: lax.rem(me_x + dx, GX) for dx in range(GX)}
+
     def to_all(act):
         def row(j, carry):
-            dy = lax.rem(j + 5, GY - 1) + 1
+            y = lax.rem(me_y + (lax.rem(j + 5, GY - 1) + 1), GY)
             for dx in (4, 3, 5, 2, 6, 1, 7, 0):
-                act(dx, dy)
+                act((columns[dx], y))
             return carry
 
         lax.fori_loop(0, GY - 1, row, 0)
         for dx in (4, 3, 5, 2, 6, 1, 7):
-            act(dx, 0)
+            act((columns[dx], me_y))
 
     pairs = [
         (pt_h, obs_pt),
@@ -507,13 +509,13 @@
         ar_src[a] = row
         arx[a, pl.ds(me, 1), :] = row
 
-        def send(dx, dy):
+        def send(device):
             pltpu.make_async_remote_copy(
                 src_ref=ar_src.at[a],
                 dst_ref=arx.at[a, pl.ds(me, 1)],
                 send_sem=as_sem.at[a],
                 recv_sem=ar_sem.at[a],
-                device_id=at(dx, dy),
+                device_id=device,
                 device_id_type=MESH,
             ).start()
 
@@ -584,7 +586,6 @@
     hit_c[1] = jnp.where(mine & (pair == 1), 1.0, 0.0)
     for k in range(18):
         jct[k] = sorted_t(jc[k] * valid, 1)
-    diag = put_cams([jct[k] * jct[k] + jct[CPAR + k] * jct[CPAR + k] for k in range(CPAR)])
     cost_row = lane_sum(rs[...] * rs[...])
     hess = collect_wait(6, *pts_h)
     for c in range(6):
@@ -619,6 +620,7 @@
     w0 = apply_inverse(inv, three(ybuf, 0))
     wbuf[0] = jnp.stack(w0)
     spread_start(w0, *out_s)
+    diag = put_cams([jct[k] * jct[k] + jct[CPAR + k] * jct[CPAR + k] for k in range(CPAR)])
     inv = invert(hess, LAMBDAS[1])
     for c in range(6):
         inv_b[1, c] = inv[c]
@@ -714,12 +716,9 @@
         ybuf[2] = jnp.stack(y)
         w = apply_inverse([inv_b[step, c] for c in range(6)], y)
         wbuf[2] = jnp.stack(w)
-        if last:
-            spread_start(w, *out_s)
-        else:
+        if not last:
             held.append([scale[m] * w[m] + y[m] for m in range(3)])
             ahead.append(apply_inverse(inv_next, held[2]))
-            spread_start([-alpha * (ahead[2][m] + w[m]) for m in range(3)], *out_s)
         y_turn = mix(1.0, three(ybuf, 1), -alpha, y)
         w_turn = mix(1.0, three(wbuf, 1), -alpha, w)
         yw = inner(y_turn, w_turn)
@@ -735,12 +734,16 @@
                 turn_sq - 2.0 * yw + inner(w_turn, hw_turn),
             ]
         total_start(step, rows)
+        if last:
+            spread_start(w, *out_s)
+        else:
+            spread_start([-alpha * (ahead[2][m] + w[m]) for m in range(3)], *out_s)
         if not last:
-            spread_start(w, *out_2)
             spread_wait(*out_w)
             near_fix = take_points(recv_w)
             near_one = take_points(recv_w, 3)
             spread_wait(*out_s)
+            spread_start(w, *out_2)
             near_move = take_points(recv_s)
         else:
             spread_wait(*out_s)

time: 79.7 us -> 78.1 us (0.980)
  Pallas kernels: 78.9 us -> 77.3 us
    pallas_call x1, Pallas kernels: 77.3 us -> 75.7 us  [body(): pl.pallas_call(kernel, out_shape=shapes, in_specs=[pl.BlockSpec(memory_sp...]
where the time goes in v7:
time: 78.1 us; the launch traced here: 78 us
  Pallas kernels  77.3 us (99%)
    pallas_call x1, Pallas kernels, body(): pl.pallas_call(kernel, out_shape=shapes, in_specs=[pl.BlockSpec(memory_sp...  75.7 us
    pallas_call x1, Pallas kernels, body(): pl.pallas_call(hand_over, out_shape=shapes, in_specs=[vmem] * 4, out_spec...  1.62 us

profile of v7, /device:TPU:1, one launch (start us, length us, event | category | flops | bytes accessed | tf_op | source)
XLA Modules:
  0.0 78.0 jit_solution(2765263899257008758)
XLA Ops:
  0.6 75.7 %shard_map.138 = (f32[9,4,64]{2,1,0:T(4,128)}, f32[3,16,128]{2,1,0:T(8,128)}, f32[256,128]{1,0:T(8,128)}, f32[1,3]{1,0:T(1,128)}) custom-call(s32[128]{0:T(128)} %bitcast.38, f32[18,128,128]{2,1,0:T(8,128)} %bitcast.30, f32[6,128,128]{2,1,0:T(8,128)} %bitcast.31, f32[256,128]{1,0:T(8,128)} %bitcast.32, s32[128,128]{1,0:T(8,128)} %bitcast.33, ...), custom_call_target="tpu_custom_call" | custom-call | tf_op jit(solution)/shard_map/pallas_call | solution.py:833
  76.4 1.6 %shard_map.139 = (f32[9,4,64]{2,1,0:T(4,128)}, f32[3,16,128]{2,1,0:T(8,128)}, f32[256,128]{1,0:T(8,128)}, f32[1,3]{1,0:T(1,128)}) custom-call(f32[9,4,64]{2,1,0:T(4,128)} %get-tuple-element.12.cam_i, f32[3,16,128]{2,1,0:T(8,128)} %get-tuple-element.13.pt_i, f32[256,128]{1,0:T(8,128)} %get-tuple-element.14.res_i, f32[1,3]{1,0:T(1,128)} %get-tuple-element.15.cost_i), custom_call_target="tpu_custom_call" | custom-call | tf_op jit(solution)/shard_map/pallas_call | solution.py:915

commit v8 on v7

--- a/solution.py
+++ b/solution.py
@@ -13,6 +13,7 @@
 SLOTS = 9 * NBLK
 GX = 8
 GY = 16
+CHIPS = GX * GY // 2
 PAD = 64
 STEPS = (1, 2, 4, 8, 16, 32, 64)
 LAMBDAS = (1.0, 0.25)
@@ -184,6 +185,8 @@
     wbuf,
     camvec,
     camacc,
+    pair_src,
+    pair_dst,
     ar_src,
     arx,
     px_src,
@@ -204,6 +207,8 @@
     wr_sem,
     s2_sem,
     r2_sem,
+    ps_sem,
+    pr_sem,
     as_sem,
     ar_sem,
     pxs_sem,
@@ -224,17 +229,19 @@
         x, y = me_x + (a - 1), me_y + (b - 1)
         here[n] = (x >= 0) & (x < GX) & (y >= 0) & (y < GY)
 
-    columns = {dx: lax.rem(me_x + dx, GX) for dx in range(GX)}
-
-    def to_all(act):
+    partner = (me_x + 1 - 2 * lax.rem(me_x, 2), me_y)
+    chip = (me_x // 2) * GY + me_y
+    columns = {dx: lax.rem(me_x + dx, GX) for dx in range(0, GX, 2)}
+
+    def to_chips(act):
         def row(j, carry):
             y = lax.rem(me_y + (lax.rem(j + 5, GY - 1) + 1), GY)
-            for dx in (4, 3, 5, 2, 6, 1, 7, 0):
+            for dx in (4, 2, 6, 0):
                 act((columns[dx], y))
             return carry
 
         lax.fori_loop(0, GY - 1, row, 0)
-        for dx in (4, 3, 5, 2, 6, 1, 7):
+        for dx in (4, 2, 6):
             act((columns[dx], me_y))
 
     pairs = [
@@ -506,31 +513,43 @@
 
     def total_start(a, rows):
         row = lane_row(rows)
+        pair_src[a] = row
+        pltpu.make_async_remote_copy(
+            src_ref=pair_src.at[a],
+            dst_ref=pair_dst.at[a],
+            send_sem=ps_sem.at[a],
+            recv_sem=pr_sem.at[a],
+            device_id=partner,
+            device_id_type=MESH,
+        ).start()
+
+    def total_turn(a):
+        pltpu.make_async_copy(pair_src.at[a], pair_dst.at[a], pr_sem.at[a]).wait()
+        row = pair_src[a] + pair_dst[a]
         ar_src[a] = row
-        arx[a, pl.ds(me, 1), :] = row
+        arx[a, pl.ds(chip, 1), :] = row
 
         def send(device):
             pltpu.make_async_remote_copy(
                 src_ref=ar_src.at[a],
-                dst_ref=arx.at[a, pl.ds(me, 1)],
+                dst_ref=arx.at[a, pl.ds(chip, 1)],
                 send_sem=as_sem.at[a],
                 recv_sem=ar_sem.at[a],
                 device_id=device,
                 device_id_type=MESH,
             ).start()
 
-        to_all(send)
+        to_chips(send)
 
     def total_wait(a):
-        pltpu.make_async_copy(
-            arx.at[a, pl.ds(0, 127)], arx.at[a, pl.ds(0, 127)], ar_sem.at[a]
-        ).wait()
+        rest = arx.at[a, pl.ds(0, CHIPS - 1)]
+        pltpu.make_async_copy(rest, rest, ar_sem.at[a]).wait()
         return apart(jnp.sum(arx[a], axis=0, keepdims=True), 9)
 
     def total_drain(a):
-        pltpu.make_async_copy(
-            arx.at[a, pl.ds(0, 127)], arx.at[a, pl.ds(0, 127)], as_sem.at[a]
-        ).wait()
+        pltpu.make_async_copy(pair_src.at[a], pair_dst.at[a], ps_sem.at[a]).wait()
+        rest = arx.at[a, pl.ds(0, CHIPS - 1)]
+        pltpu.make_async_copy(rest, rest, as_sem.at[a]).wait()
 
     copies[0].wait()
     hit_p[...] = jnp.where(order(0, obs_pt[...], lane), 1.0, 0.0)
@@ -716,9 +735,6 @@
         ybuf[2] = jnp.stack(y)
         w = apply_inverse([inv_b[step, c] for c in range(6)], y)
         wbuf[2] = jnp.stack(w)
-        if not last:
-            held.append([scale[m] * w[m] + y[m] for m in range(3)])
-            ahead.append(apply_inverse(inv_next, held[2]))
         y_turn = mix(1.0, three(ybuf, 1), -alpha, y)
         w_turn = mix(1.0, three(wbuf, 1), -alpha, w)
         yw = inner(y_turn, w_turn)
@@ -734,10 +750,15 @@
                 turn_sq - 2.0 * yw + inner(w_turn, hw_turn),
             ]
         total_start(step, rows)
+        if not last:
+            held.append([scale[m] * w[m] + y[m] for m in range(3)])
+            ahead.append(apply_inverse(inv_next, held[2]))
+            w_move = [-alpha * (ahead[2][m] + w[m]) for m in range(3)]
+        total_turn(step)
         if last:
             spread_start(w, *out_s)
         else:
-            spread_start([-alpha * (ahead[2][m] + w[m]) for m in range(3)], *out_s)
+            spread_start(w_move, *out_s)
         if not last:
             spread_wait(*out_w)
             near_fix = take_points(recv_w)
@@ -885,7 +906,9 @@
             pltpu.VMEM((CPAR, 2, LANES), F32),
             pltpu.VMEM((CPAR, 2, LANES), F32),
             pltpu.VMEM((2, 1, LANES), F32),
-            pltpu.VMEM((2, GX * GY, LANES), F32),
+            pltpu.VMEM((2, 1, LANES), F32),
+            pltpu.VMEM((2, 1, LANES), F32),
+            pltpu.VMEM((2, CHIPS, LANES), F32),
             pltpu.VMEM((2, 1, LANES), F32),
             pltpu.VMEM((2, GX, LANES), F32),
             pltpu.VMEM((2, 1, LANES), F32),
@@ -894,7 +917,7 @@
             pltpu.SMEM((2, LANES), jnp.int32),
         ]
         + [dma((8,))] * 12
-        + [dma((2,))] * 6,
+        + [dma((2,))] * 8,
         compiler_params=pltpu.CompilerParams(
             collective_id=0, has_side_effects=True, vmem_limit_bytes=62 * 1024 * 1024
         ),

time: 78.1 us -> 78.3 us (level)
  no operation moved by 1% of the time
where the time goes in v8:
time: 78.3 us; the launch traced here: 78.1 us
  Pallas kernels  77.5 us (99%)
    pallas_call x1, Pallas kernels, body(): pl.pallas_call(kernel, out_shape=shapes, in_specs=[pl.BlockSpec(memory_sp...  75.9 us
    pallas_call x1, Pallas kernels, body(): pl.pallas_call(hand_over, out_shape=shapes, in_specs=[vmem] * 4, out_spec...  1.62 us

profile of v8, /device:TPU:1, one launch (start us, length us, event | category | flops | bytes accessed | tf_op | source)
XLA Modules:
  0.0 78.1 jit_solution(14126491862067006090)
XLA Ops:
  0.6 75.9 %shard_map.138 = (f32[9,4,64]{2,1,0:T(4,128)}, f32[3,16,128]{2,1,0:T(8,128)}, f32[256,128]{1,0:T(8,128)}, f32[1,3]{1,0:T(1,128)}) custom-call(s32[128]{0:T(128)} %bitcast.38, f32[18,128,128]{2,1,0:T(8,128)} %bitcast.30, f32[6,128,128]{2,1,0:T(8,128)} %bitcast.31, f32[256,128]{1,0:T(8,128)} %bitcast.32, s32[128,128]{1,0:T(8,128)} %bitcast.33, ...), custom_call_target="tpu_custom_call" | custom-call | tf_op jit(solution)/shard_map/pallas_call | solution.py:854
  76.5 1.6 %shard_map.139 = (f32[9,4,64]{2,1,0:T(4,128)}, f32[3,16,128]{2,1,0:T(8,128)}, f32[256,128]{1,0:T(8,128)}, f32[1,3]{1,0:T(1,128)}) custom-call(f32[9,4,64]{2,1,0:T(4,128)} %get-tuple-element.12.cam_i, f32[3,16,128]{2,1,0:T(8,128)} %get-tuple-element.13.pt_i, f32[256,128]{1,0:T(8,128)} %get-tuple-element.14.res_i, f32[1,3]{1,0:T(1,128)} %get-tuple-element.15.cost_i), custom_call_target="tpu_custom_call" | custom-call | tf_op jit(solution)/shard_map/pallas_call | solution.py:938
